TPU v7x, 256 devices: a whole 4x4x8 slice. The times are simulated.
256 devices in a mesh: space: 64 (over z, y, x_hi), rep: 4 (over x_lo, core).
Axes of the slice: x: 4 (x_hi: 2, x_lo: 2; x = x_hi * 2 + x_lo), y: 4, z: 8, core: 2. Of those that a mesh axis runs over, the one named last changes fastest.
Arguments:
- features: bfloat16 [1024, 64, 512], P(('space', 'rep')), may hold values from -6 to 6
- neighbours: int32 [1024, 27], P(('space', 'rep')), may hold values from -1 to 7, as said below
- counts: int32 [256], P(('space', 'rep')), may hold values from 1 to 4, as said below
- cotangent: bfloat16 [1024, 64, 128], P(('space', 'rep')), may hold values from -0.0234375 to 0.0234375
- conv_weight: bfloat16 [27, 64, 64], replicated, may hold values from -0.15625 to 0.15625
- down_weight: bfloat16 [8, 128, 64], replicated, may hold values from -0.25 to 0.25
Outputs:
- hidden: bfloat16 [1024, 64, 512], P(('space', 'rep'))
- conv_grad: float32 [27, 64, 64], replicated
- down_grad: float32 [8, 128, 64], replicated
Inputs may be any that keep to these rules, and one draw needn't show every extreme that they name: `counts`: in every tile, of the two strips s and s + 32 at most one has more than 2 occupied blocks; some strip has exactly 4 and some exactly 2. Only live slots name neighbours, and they name only live slots; strip 0 names nothing below and the last strip nothing above.
All inputs are finite; a program needn't handle non-finite values.
Results may differ from a plain program's by a relative error of at most 0.0029.
Values may be sent and summed in bfloat16 or wider, within the bound.
A program may use at most 64 MiB of HBM per device.

v0:
```python
import jax
import jax.numpy as jnp
from jax import lax
from jax.sharding import PartitionSpec as P


def from_behind(block, axis, distance):
    devices = range(lax.axis_size(axis))
    route = [(i - distance, i) for i in devices if i - distance in devices]
    return lax.ppermute(block, axis, route)


def plane_slice(offset):
    if offset < 0:
        return slice(7, 8)
    if offset > 0:
        return slice(0, 1)
    return slice(0, 8)


def take_rows(source_table, index_rows):
    padding = jnp.zeros((1,) + source_table.shape[1:], source_table.dtype)
    extended = jnp.concatenate([source_table, padding], 0)
    safe_index = jnp.where(index_rows < 0, source_table.shape[0], index_rows)
    return jnp.take(extended, safe_index, axis=0)


def build_padded(features_live, prev_upper, next_lower, neighbours):
    count_rows, channels = (features_live.shape[0], features_live.shape[1])
    blocks = features_live.reshape(count_rows, channels, 8, 8, 8)
    low_table = jnp.concatenate([blocks[:, :, 7:8], prev_upper.reshape(-1, channels, 1, 8, 8)], 0)
    high_table = jnp.concatenate([blocks[:, :, 0:1], next_lower.reshape(-1, channels, 1, 8, 8)], 0)
    layers = []
    for step_x, source_table in ((-1, low_table), (0, blocks), (1, high_table)):
        row_list = []
        for step_y in (-1, 0, 1):
            tile_list = []
            for step_z in (-1, 0, 1):
                column = (step_x + 1) * 9 + (step_y + 1) * 3 + step_z + 1
                if column == 13:
                    tile_list.append(blocks)
                else:
                    piece = source_table[:, :, :, plane_slice(step_y), plane_slice(step_z)]
                    tile_list.append(take_rows(piece, neighbours[:, column]))
            row_list.append(jnp.concatenate(tile_list, 4))
        layers.append(jnp.concatenate(row_list, 3))
    return jnp.concatenate(layers, 2)


def block_section(padded, grads_in, conv_weight, down_weight):
    count_rows, channels = (padded.shape[0], padded.shape[1])
    out_channels = down_weight.shape[1]

    def shifted_at(column):
        step_x, step_y, step_z = (column // 9 - 1, column // 3 % 3 - 1, column % 3 - 1)
        window = padded[
            :, :, 1 + step_x : 9 + step_x, 1 + step_y : 9 + step_y, 1 + step_z : 9 + step_z
        ]
        return window.reshape(count_rows, channels, 512)

    pre_act = jnp.zeros((count_rows, channels, 512), jnp.float32)
    for column in range(27):
        pre_act = pre_act + jnp.einsum(
            "oc,bcv->bov",
            conv_weight[column],
            shifted_at(column),
            preferred_element_type=jnp.float32,
        )
    hidden = jnp.maximum(pre_act, 0.0).astype(jnp.bfloat16)
    hidden_cells = hidden.reshape(count_rows, channels, 4, 2, 4, 2, 4, 2)
    grid_grads = grads_in.reshape(count_rows, 4, 4, 4, out_channels)
    down_grad = jnp.einsum(
        "bcxiyjzk,bxyzo->ijkoc", hidden_cells, grid_grads, preferred_element_type=jnp.float32
    ).reshape(8, out_channels, channels)
    kernel = down_weight.reshape(2, 2, 2, out_channels, channels)
    hidden_grad = jnp.einsum(
        "ijkoc,bxyzo->bcxiyjzk", kernel, grid_grads, preferred_element_type=jnp.float32
    ).reshape(count_rows, channels, 512)
    act_grad = jnp.where(pre_act > 0, hidden_grad, 0.0).astype(jnp.bfloat16)
    conv_grad = jnp.stack(
        [
            jnp.einsum(
                "bov,bcv->oc", act_grad, shifted_at(column), preferred_element_type=jnp.float32
            )
            for column in range(27)
        ]
    )
    return (hidden, conv_grad, down_grad)


def body(features, neighbours, counts, cotangent, conv_weight, down_weight):
    slot_count = features.shape[0]
    live_mask = (lax.iota(jnp.int32, slot_count) < counts[0])[:, None, None]
    features_live = jnp.where(live_mask, features, jnp.zeros_like(features))
    grads_live = jnp.where(live_mask, cotangent, jnp.zeros_like(cotangent))
    prev_upper = from_behind(features_live[:, :, 448:], "space", 1)
    next_lower = from_behind(features_live[:, :, :64], "space", -1)
    padded = build_padded(features_live, prev_upper, next_lower, neighbours)
    hidden, conv_grad, down_grad = block_section(padded, grads_live, conv_weight, down_weight)
    conv_grad, down_grad = lax.psum((conv_grad, down_grad), ("space", "rep"))
    return (hidden, conv_grad, down_grad)


def solution(mesh):
    return jax.shard_map(
        body,
        mesh=mesh,
        in_specs=(
            P(("space", "rep"), None, None),
            P(("space", "rep"), None),
            P(("space", "rep")),
            P(("space", "rep"), None, None),
            P(),
            P(),
        ),
        out_specs=(P(("space", "rep"), None, None), P(), P()),
        check_vma=False,
    )
```

profile of v0, /device:TPU:1, one launch (start us, length us, event | category | flops | bytes accessed | tf_op | source)
XLA Modules:
  0.0 418.5 jit_solution(137466216667750516)
XLA Ops:
  7.9 1.0 broadcast_select_fusion
  9.7 6.1 %collective-permute-start = (bf16[4,64,64]{2,1,0:T(8,128)(2,1)}, bf16[4,64,64]{2,1,0:T(8,128)(2,1)}, u32[]{:S(2)}, u32[]{:S(2)}) collective-permute-start(bf16[4,64,64]{2,1,0:T(8,128)(2,1)} %get-tuple-element.130), channel_id=1, source_target_pairs={{0,4},{4,8},{8,12},{12,16},{16,20},{20,24},{24,28},{28,32},{32,36}... | collective-permute-start | bytes 98312 | tf_op jit(solution)/shard_map/ppermute | solution.py:10
  15.8 1.3 collective-permute-start.1
  33.9 1.6 maximum_maximum_fusion.3
  45.6 0.9 copy.91
  46.5 0.9 copy.93
  47.4 0.9 copy.95
  48.9 0.9 copy.105
  50.3 0.9 copy.137
  51.3 0.9 copy.46
  52.3 1.0 copy.107
  55.3 1.0 maximum_bitcast_fusion
  69.8 0.8 gather_fusion.4
  72.2 3.6 maximum_maximum_fusion
  75.8 2.6 fusion.160
  79.6 1.2 copy-done.42
  87.0 1.0 convolution_add_fusion
  105.2 6.5 %maximum_maximum_fusion.1 = bf16[4,64,9,10,10]{1,0,4,3,2:T(4,128)(2,1)S(1)} fusion(bf16[4,64,1,1,1]{1,0,4,3,2:T(4,128)(2,1)S(1)} %bitcast_select_fusion.18, bf16[4,64,1,1,8]{1,0,4,3,2:T(4,128)(2,1)S(1)} %bitcast_select_fusion.6, bf16[4,64,1,1,1]{1,0,4,3,2:T(4,128)(2,1)S(1)} %copy-done.61, bf16[4,64,1,8,1]{1,0,4,3,2:T(4,128)(2,1)S(1)} %bitcast_select_fusion.7, ...), kind=kLoop, calls=%fused_computation.119 | loop fusion | flops 3916800 | bytes 921600 | tf_op jit(solution)/shard_map/concatenate | solution.py:47
  111.7 2.8 fusion.159
  114.6 1.0 convolution_bitcast_fusion.7
  115.8 1.0 convolution_bitcast_fusion.8
  116.9 1.0 convolution_bitcast_fusion.9
  118.0 1.0 convolution_bitcast_fusion.3
  119.2 1.0 convolution_bitcast_fusion.4
  120.3 1.0 convolution_bitcast_fusion.5
  121.6 1.0 convolution_bitcast_fusion.1
  122.7 0.9 copy-done.26
  123.7 1.0 convolution_add_fusion.3
  124.7 1.0 convolution_add_fusion.2
  125.7 1.1 fusion.10
  126.8 1.0 fusion.3
  127.8 1.1 fusion.7
  128.9 1.1 select_convert_fusion
  130.3 0.9 copy-done.22
  131.4 0.8 copy-done.20
  132.4 0.8 copy-done.18
  133.5 0.8 copy-done.16
  134.5 0.8 copy-done.14
  135.6 0.8 copy-done.12
  136.6 0.8 copy-done.8
  137.7 0.8 copy-done.10
  138.7 0.8 copy-done.6
  139.7 0.8 copy-done.2
  140.8 0.8 copy-done.4
  145.3 0.9 copy-done.41
  147.1 1.2 fusion.38
  148.3 260.4 %all-reduce.27.cloned.1.call-done = (f32[27,64,64]{2,1,0:T(8,128)}, f32[8,128,64]{1,2,0:T(8,128)}) async-done(((f32[27,64,64]{2,1,0:T(8,128)}, f32[8,128,64]{1,2,0:T(8,128)}), (f32[27,64,64]{2,1,0:T(8,128)}, f32[8,128,64]{1,2,0:T(8,128)})) %all-reduce.27.cloned.1.call-update) | async-done | bytes 704528 | tf_op jit(solution)/shard_map/psum | solution.py:100
  408.7 2.2 copy.271
  (349 shorter events, 78.2 us)
Async XLA Ops:
  7.2 37.5 %copy-start = (bf16[8,128,64]{1,2,0:T(8,128)(2,1)S(1)}, bf16[8,128,64]{1,2,0:T(8,128)(2,1)}, u32[]{:S(2)}) copy-start(bf16[8,128,64]{1,2,0:T(8,128)(2,1)} %param.25) | copy-start | bytes 393220
  7.2 401.5 %all-reduce.27.cloned.1.call-start = ((), (), s32[]{:S(2)}) async-start(), calls=%async_computation | async-start | bytes 2293760 | tf_op jit(solution)/shard_map/psum | solution.py:100
  9.7 41.6 %collective-permute-start = (bf16[4,64,64]{2,1,0:T(8,128)(2,1)}, bf16[4,64,64]{2,1,0:T(8,128)(2,1)}, u32[]{:S(2)}, u32[]{:S(2)}) collective-permute-start(bf16[4,64,64]{2,1,0:T(8,128)(2,1)} %get-tuple-element.130), channel_id=1, source_target_pairs={{0,4},{4,8},{8,12},{12,16},{16,20},{20,24},{24,28},{28,32},{32,36}... | collective-permute-start | bytes 98312 | tf_op jit(solution)/shard_map/ppermute | solution.py:10
  15.8 36.5 %collective-permute-start.1 = (bf16[4,64,64]{2,1,0:T(8,128)(2,1)}, bf16[4,64,64]{2,1,0:T(8,128)(2,1)}, u32[]{:S(2)}, u32[]{:S(2)}) collective-permute-start(bf16[4,64,64]{2,1,0:T(8,128)(2,1)} %get-tuple-element.131), channel_id=1, source_target_pairs={{4,0},{8,4},{12,8},{16,12},{20,16},{24,20},{28,24},{32,28},{36,32}... | collective-permute-start | bytes 98312 | tf_op jit(solution)/shard_map/ppermute | solution.py:10
  29.9 3.9 copy-start.46
  30.5 3.3 copy-start.48
  31.2 2.6 copy-start.27
  31.9 1.9 copy-start.29
  32.6 1.3 copy-start.36
  36.3 5.2 %copy-start.55 = (bf16[4,64,128]{2,1,0:T(8,128)(2,1)S(1)}, bf16[4,64,128]{2,1,0:T(8,128)(2,1)}, u32[]{:S(2)}) copy-start(bf16[4,64,128]{2,1,0:T(8,128)(2,1)} %param.23) | copy-start | bytes 196612
  41.6 3.4 copy-start.44
  69.8 1.6 copy-start.37
  69.8 1.6 copy-start.39
  69.8 1.6 copy-start.47
  69.8 1.6 copy-start.49
  78.5 1.1 copy-start.23
  78.6 2.4 copy-start.21
  78.8 2.6 copy-start.19
  78.9 2.8 copy-start.17
  79.0 3.0 copy-start.15
  79.1 3.1 copy-start.13
  79.3 3.3 copy-start.11
  79.4 3.5 copy-start.7
  79.4 1.3 copy-start.42
  79.6 3.7 copy-start.9
  83.2 1.0 copy-start.5
  84.3 1.0 copy-start.1
  85.3 1.0 copy-start.3
  87.0 1.8 copy-start.40
  88.8 2.1 copy-start.80
  88.8 3.5 copy-start.81
  103.1 1.5 copy-start.61
  103.1 1.5 copy-start.62
  103.1 1.5 copy-start.63
  122.6 1.0 copy-start.26
  125.7 1.1 copy-start.25
  127.8 1.1 copy-start.34
  128.9 1.1 copy-start.24
  130.0 16.2 %copy-start.35 = (bf16[4,64,512]{2,1,0:T(8,128)(2,1)}, bf16[4,64,512]{2,1,0:T(8,128)(2,1)S(1)}, u32[]{:S(2)}) copy-start(bf16[4,64,512]{2,1,0:T(8,128)(2,1)S(1)} %get-tuple-element.192) | copy-start | bytes 786436
  130.0 1.1 copy-start.22
  131.2 1.0 copy-start.20
  132.2 1.0 copy-start.18
  133.3 1.0 copy-start.16
  134.3 1.0 copy-start.14
  135.3 1.0 copy-start.12
  136.4 1.0 copy-start.8
  137.4 1.0 copy-start.10
  408.7 2.2 copy-start.43
  (37 other events, 27.6 us)
Sparse Core Ops, SparseCore 0:
  148.4 260.2 all-reduce.26
where the time goes:
time: 421 us; the launch traced here: 418 us
  waiting for transfers between devices  260 us (62%)
  local copies, waits for them, and re-layouts  69.6 us (17%)
  other arithmetic  39 us (9%)
  matrix products  25.8 us (6%)
  between operations  16.3 us (4%)
  starting transfers between devices  7.41 us (2%)
    psum x1, waiting for transfers between devices, body(): conv_grad, down_grad = lax.psum((conv_grad, down_grad), ('space', 'rep'))  260 us
    unnamed x166, local copies, waits for them, and re-layouts  32.6 us
    dot_general x27, matrix products, block_section(): jnp.einsum('oc,bcv->bov', conv_weight[column], shifted_at(column), prefer...  18.3 us
    gather x26, local copies, waits for them, and re-layouts, take_rows(): return jnp.take(extended, safe_index, axis=0)  17 us
    slice x30, local copies, waits for them, and re-layouts, shifted_at(): padded[:, :, 1 + step_x:9 + step_x, 1 + step_y:9 + step_y, 1 + step_z:9 +...  13.2 us
    concatenate x2, other arithmetic, build_padded(): return jnp.concatenate(layers, 2)  10 us
    and x23, other arithmetic, take_rows(): return jnp.take(extended, safe_index, axis=0)  8.5 us
  transfers between devices with their start and end apart: 3, of which 1 were waited for; matrix products, arithmetic and copies ran while one was open for 8% of the time, Pallas kernels for 0%

commit v1 on v0

v1 whole, which is shorter than its diff:
```python
import functools

import jax
import jax.numpy as jnp
from jax import lax
from jax.experimental import pallas as pl
from jax.experimental.pallas import tpu as pltpu
from jax.sharding import PartitionSpec as P

MESH = pl.DeviceIdType.MESH
F32, BF16 = jnp.float32, jnp.bfloat16
VM = pl.BlockSpec(memory_space=pltpu.VMEM)
SM = pl.BlockSpec(memory_space=pltpu.SMEM)
NX, NY, NZ = 4, 4, 8
NXY = NX * NY
CONV_ROWS, DOWN_ROWS = 32, 16
ROWS = CONV_ROWS + DOWN_ROWS


def dot(a, b, dims):
    return lax.dot_general(a, b, (dims, ((), ())), preferred_element_type=F32)


NN, NT, TN = ((1,), (0,)), ((1,), (1,)), ((0,), (0,))


def voxels_in_rows(block):
    wide = block.astype(F32)
    return jnp.concatenate([wide, wide], 0).T


def fill_weights(cw_ref, dw_ref, w_ref, dt_ref):
    for dy in range(3):
        for dx in range(3):
            row = [cw_ref[dx * 9 + dy * 3 + dz].astype(F32) for dz in range(3)]
            w_ref[dy, dx * 64 : dx * 64 + 64, :] = jnp.concatenate(row, 1).astype(BF16)
    for t in range(0, 8, 2):
        pair = jnp.concatenate([dw_ref[t], dw_ref[t + 1]], 0).astype(F32)
        dt_ref[:, t * 128 : t * 128 + 256] = pair.T.astype(BF16)


def fill_tables(f_ref, t_ref, lo_ref, hi_ref):
    for j in range(4):
        for q in range(4):
            part = voxels_in_rows(f_ref[j, :, q * 128 : q * 128 + 128])
            t_ref[j, q * 2 : q * 2 + 2] = part.reshape(2, 8, 8, 128)
        lo_ref[j] = t_ref[j, 7]
        hi_ref[j] = t_ref[j, 0]
    t_ref[4] = jnp.zeros((8, 8, 8, 128), F32)
    lo_ref[8] = jnp.zeros((8, 8, 128), F32)
    hi_ref[8] = jnp.zeros((8, 8, 128), F32)


def fill_halo(prev_ref, next_ref, lo_ref, hi_ref):
    for j in range(4):
        lo_ref[4 + j] = voxels_in_rows(prev_ref[j])[64:].reshape(8, 8, 128)
        hi_ref[4 + j] = voxels_in_rows(next_ref[j])[:64].reshape(8, 8, 128)


def store_plane(q_ref, b, xp, middle, below, above):
    z = lax.broadcasted_iota(jnp.int32, (10, 8, 128), 1)
    first = lax.broadcasted_iota(jnp.int32, (10, 8, 128), 2) < 64
    minus = pltpu.roll(jnp.where(z == 7, below, middle), 1, 1)
    plus = pltpu.roll(jnp.where(z == 0, above, middle), 7, 1)
    left = jnp.where(first, minus, middle)
    for dy in range(3):
        rows = slice(xp * 64, xp * 64 + 64)
        q_ref[b, dy, rows, 0:128] = left[dy : dy + 8].reshape(64, 128).astype(BF16)
        q_ref[b, dy, rows, 128:256] = plus[dy : dy + 8].reshape(64, 128).astype(BF16)


def link(nb_ref, b, ox, oy, oz, zero):
    j = nb_ref[b, (ox + 1) * 9 + (oy + 1) * 3 + oz + 1]
    return jnp.where(j < 0, zero, j)


def fill_inner(nb_ref, count, b, t_ref, q_ref):
    own = jnp.where(b < count, b, 4)
    idx = [[link(nb_ref, b, 0, oy, oz, 4) for oy in (-1, 0, 1)] for oz in (0, -1, 1)]
    idx[0][1] = own
    for xp in range(1, 9):
        cols = [
            jnp.concatenate(
                [t_ref[i0, xp - 1, 7:8], t_ref[i1, xp - 1], t_ref[i2, xp - 1, 0:1]], 0
            )
            for i0, i1, i2 in idx
        ]
        store_plane(q_ref, b, xp, *cols)


def fill_outer(nb_ref, b, lo_ref, hi_ref, q_ref):
    for ox, xp, table in ((-1, 0, lo_ref), (1, 9, hi_ref)):
        cols = []
        for oz in (0, -1, 1):
            i0, i1, i2 = [link(nb_ref, b, ox, oy, oz, 8) for oy in (-1, 0, 1)]
            cols.append(jnp.concatenate([table[i0, 7:8], table[i1], table[i2, 0:1]], 0))
        store_plane(q_ref, b, xp, *cols)


def expand_cotangent(g_ref, count, b, gexp_ref):
    v = lax.broadcasted_iota(jnp.int32, (64, 512), 1)
    u = lax.broadcasted_iota(jnp.int32, (64, 512), 0)
    cell = (v // 128) * 16 + (v // 16 % 4) * 4 + v % 8 // 2
    spread = (cell == u).astype(F32).astype(BF16)
    grads = jnp.where(b < count, g_ref[b].astype(F32), 0.0)
    up = dot(grads.T.astype(BF16), spread, NN)
    w = lax.broadcasted_iota(jnp.int32, (128, 512), 1)
    place = (w // 64 % 2) * 4 + (w // 8 % 2) * 2 + w % 2
    for t in range(8):
        gexp_ref[t * 128 : t * 128 + 128] = jnp.where(place == t, up, 0.0).astype(BF16)


def block_math(b, w_ref, dt_ref, q_ref, gexp_ref, hid_ref, cg_ref, dg_ref):
    acc = jnp.zeros((192, 640), F32)
    for dy in range(3):
        acc += dot(w_ref[dy], q_ref[b, dy, :, 0:192], NT)
    pre = acc[0:64, 0:512] + acc[64:128, 64:576] + acc[128:192, 128:640]
    hidden = jnp.maximum(pre, 0.0).astype(BF16)
    hid_ref[b] = hidden
    dg_ref[...] += dot(gexp_ref[...], hidden, NT)
    grad = dot(dt_ref[...], gexp_ref[...], NN)
    act = jnp.where(pre > 0, grad, 0.0)
    gap = jnp.zeros((64, 64), F32)
    shifted = jnp.concatenate(
        [
            jnp.concatenate([act, gap, gap], 1),
            jnp.concatenate([gap, act, gap], 1),
            jnp.concatenate([gap, gap, act], 1),
        ],
        0,
    ).astype(BF16)
    for dy in range(3):
        cg_ref[dy] += dot(shifted, q_ref[b, dy], NN)


def pack(cg_ref, dg_ref, v_ref):
    def put(at, rows):
        for i in range(0, rows.shape[0], CONV_ROWS):
            v_ref[(at + i) // CONV_ROWS, 0:CONV_ROWS] = rows[i : i + CONV_ROWS]

    for dy in range(3):
        put(dy * 192, cg_ref[dy, :, 0:128])
    first = lax.broadcasted_iota(jnp.int32, (192, 128), 1) < 64
    put(576, jnp.where(first, cg_ref[0, :, 128:256], cg_ref[1, :, 128:256]))
    put(768, cg_ref[2, :, 128:256])
    put(960, jnp.zeros((64, 128), F32))
    pairs = jnp.concatenate([dg_ref[0:512], dg_ref[512:1024]], 1)
    for p in range(32):
        v_ref[p, CONV_ROWS:ROWS] = pairs[p * 16 : p * 16 + 16]


def local_kernel(
    nb_ref, cnt_ref, f_ref, prev_ref, next_ref, g_ref, cw_ref, dw_ref, hid_ref, v_ref,
    t_ref, lo_ref, hi_ref, q_ref, w_ref, dt_ref, gexp_ref, cg_ref, dg_ref,
):
    count = cnt_ref[0]
    fill_weights(cw_ref, dw_ref, w_ref, dt_ref)
    fill_tables(f_ref, t_ref, lo_ref, hi_ref)
    fill_halo(prev_ref, next_ref, lo_ref, hi_ref)
    cg_ref[...] = jnp.zeros(cg_ref.shape, F32)
    dg_ref[...] = jnp.zeros(dg_ref.shape, F32)
    for b in range(4):
        fill_inner(nb_ref, count, b, t_ref, q_ref)
        fill_outer(nb_ref, b, lo_ref, hi_ref, q_ref)
        expand_cotangent(g_ref, count, b, gexp_ref)
        block_math(b, w_ref, dt_ref, q_ref, gexp_ref, hid_ref, cg_ref, dg_ref)
    pack(cg_ref, dg_ref, v_ref)


def local_math(features, neighbours, counts, cotangent, conv_weight, down_weight, prev, after):
    return pl.pallas_call(
        local_kernel,
        out_shape=(
            jax.ShapeDtypeStruct((4, 64, 512), BF16),
            jax.ShapeDtypeStruct((32, ROWS, 128), F32),
        ),
        in_specs=[SM, SM, VM, VM, VM, VM, VM, VM],
        out_specs=(VM, VM),
        scratch_shapes=[
            pltpu.VMEM((5, 8, 8, 8, 128), F32),
            pltpu.VMEM((9, 8, 8, 128), F32),
            pltpu.VMEM((9, 8, 8, 128), F32),
            pltpu.VMEM((4, 3, 640, 256), BF16),
            pltpu.VMEM((3, 192, 192), BF16),
            pltpu.VMEM((64, 1024), BF16),
            pltpu.VMEM((1024, 512), BF16),
            pltpu.VMEM((3, 192, 256), F32),
            pltpu.VMEM((1024, 64), F32),
        ],
        compiler_params=pltpu.CompilerParams(vmem_limit_bytes=48 << 20),
        name="local_math",
    )(neighbours, counts, features, prev, after, cotangent, conv_weight, down_weight)


def position():
    s, r = lax.axis_index("space"), lax.axis_index("rep")
    return s // 8, s // 2 % 4, s % 2 * 2 + r // 2, r % 2


def device(z, y, x, core):
    return {"space": z * 8 + y * 2 + x // 2, "rep": x % 2 * 2 + core}


def reduce_kernel(v_ref, o_ref, mate, outgoing, parts, along, gathered, ss, rs, zs, zr, gs, gr, cs, cr):
    z, y, x, core = position()
    me = y * NX + x
    sibling = device(z, y, x, 1 - core)
    plane = [((dy, dx)) for dy in range(NY) for dx in range(NX) if dy or dx]
    plane.sort(key=lambda o: -(min(o[0], NY - o[0]) + min(o[1], NX - o[1])))

    def plane_peer(o):
        py, px = (y + o[0]) % NY, (x + o[1]) % NX
        return device(z, py, px, core), py * NX + px

    def line_peer(dz):
        return device((z + dz) % NZ, y, x, core)

    barrier = pltpu.get_barrier_semaphore()
    greet = [sibling] + [plane_peer(o)[0] for o in plane] + [line_peer(d) for d in range(1, NZ)]
    for d in greet:
        pl.semaphore_signal(barrier, inc=1, device_id=d, device_id_type=MESH)
    pl.semaphore_wait(barrier, len(greet))

    half = pltpu.make_async_remote_copy(
        v_ref.at[pl.ds((1 - core) * NXY, NXY)], mate, cs.at[0], cr.at[0],
        device_id=sibling, device_id_type=MESH,
    )
    half.start()
    half.wait()
    mine = v_ref[pl.ds(core * NXY, NXY)] + mate[...]
    mate[...] = mine
    outgoing[...] = mine.astype(BF16)

    copies = []
    for i, o in enumerate(plane):
        peer, at = plane_peer(o)
        copies.append(
            pltpu.make_async_remote_copy(
                outgoing.at[at], parts.at[i], ss.at[i], rs.at[i],
                device_id=peer, device_id_type=MESH,
            )
        )
        copies[-1].start()
    total = mate[me]
    for i, c in enumerate(copies):
        c.wait_recv()
        total = total + parts[i].astype(F32)
    for c in copies:
        c.wait_send()

    along[z] = total.astype(BF16)
    copies = []
    for i, dz in enumerate((4, 3, 5, 2, 6, 1, 7)):
        copies.append(
            pltpu.make_async_remote_copy(
                along.at[z], along.at[z], zs.at[i], zr.at[i],
                device_id=line_peer(dz), device_id_type=MESH,
            )
        )
        copies[-1].start()
    for c in copies:
        c.wait()
    total = along[0].astype(F32)
    for i in range(1, NZ):
        total = total + along[i].astype(F32)

    gathered[core, me] = total
    copies = []
    for i, o in enumerate(plane):
        peer, _ = plane_peer(o)
        copies.append(
            pltpu.make_async_remote_copy(
                gathered.at[core, me], gathered.at[core, me], gs.at[i], gr.at[i],
                device_id=peer, device_id_type=MESH,
            )
        )
        copies[-1].start()
    for c in copies:
        c.wait()
    rest = pltpu.make_async_remote_copy(
        gathered.at[core], gathered.at[core], cs.at[1], cr.at[1],
        device_id=sibling, device_id_type=MESH,
    )
    rest.start()
    rest.wait()
    o_ref[...] = gathered[...].reshape(o_ref.shape)


def reduce_all(pieces):
    dma = pltpu.SemaphoreType.DMA
    return pl.pallas_call(
        reduce_kernel,
        out_shape=jax.ShapeDtypeStruct((32, ROWS, 128), F32),
        in_specs=[VM],
        out_specs=VM,
        scratch_shapes=[
            pltpu.VMEM((NXY, ROWS, 128), F32),
            pltpu.VMEM((NXY, ROWS, 128), BF16),
            pltpu.VMEM((NXY - 1, ROWS, 128), BF16),
            pltpu.VMEM((NZ, ROWS, 128), BF16),
            pltpu.VMEM((2, NXY, ROWS, 128), F32),
            dma((NXY - 1,)), dma((NXY - 1,)), dma((NZ - 1,)), dma((NZ - 1,)),
            dma((NXY - 1,)), dma((NXY - 1,)), dma((2,)), dma((2,)),
        ],
        compiler_params=pltpu.CompilerParams(
            collective_id=0, has_side_effects=True, vmem_limit_bytes=48 << 20
        ),
        name="reduce_all",
    )(pieces)


def unpack_kernel(v_ref, conv_ref, down_ref):
    conv = v_ref[:, 0:CONV_ROWS].reshape(1024, 128)
    for dy in range(3):
        for dx in range(3):
            at = dy * 192 + dx * 64
            pair = conv[at : at + 64]
            conv_ref[dx * 9 + dy * 3] = pair[:, 0:64]
            conv_ref[dx * 9 + dy * 3 + 1] = pair[:, 64:128]
            at = 768 + dx * 64 if dy == 2 else 576 + dx * 64
            side = 64 if dy == 1 else 0
            conv_ref[dx * 9 + dy * 3 + 2] = conv[at : at + 64, side : side + 64]
    down = v_ref[:, CONV_ROWS:ROWS].reshape(512, 128)
    for t in range(8):
        rows = down[t % 4 * 128 : t % 4 * 128 + 128]
        down_ref[t] = rows[:, t // 4 * 64 : t // 4 * 64 + 64]


def unpack(pieces):
    return pl.pallas_call(
        unpack_kernel,
        out_shape=(
            jax.ShapeDtypeStruct((27, 64, 64), F32),
            jax.ShapeDtypeStruct((8, 128, 64), F32),
        ),
        in_specs=[VM],
        out_specs=(VM, VM),
        name="unpack",
    )(pieces)


def shift_strip(planes, distance):
    n = lax.axis_size("space")
    route = [(i, i + distance) for i in range(n) if 0 <= i + distance < n]
    return lax.ppermute(planes, "space", route)


def body(features, neighbours, counts, cotangent, conv_weight, down_weight):
    prev = shift_strip(features[:, :, 384:], 1)
    after = shift_strip(features[:, :, :128], -1)
    hidden, pieces = local_math(
        features, neighbours, counts, cotangent, conv_weight, down_weight, prev, after
    )
    conv_grad, down_grad = unpack(reduce_all(pieces))
    return hidden, conv_grad, down_grad


def solution(mesh):
    both = ("space", "rep")
    return jax.shard_map(
        body,
        mesh=mesh,
        in_specs=(
            P(both, None, None), P(both, None), P(both), P(both, None, None), P(), P(),
        ),
        out_specs=(P(both, None, None), P(), P()),
        check_vma=False,
    )
```

time: 421 us -> 61.9 us (0.15)
  waiting for transfers between devices: 260 us -> 0.44 us
  local copies, waits for them, and re-layouts: 69.6 us -> 5.12 us
  Pallas kernels: 0 us -> 47.1 us
  other arithmetic: 39 us -> 0 us
  matrix products: 25.8 us -> 0 us
  between operations: 16.3 us -> 1.38 us
    psum x1 -> x0, waiting for transfers between devices: 260 us -> none  [body(): conv_grad, down_grad = lax.psum((conv_grad, down_grad), ('space', 'rep'))]
    pallas_call x0 -> x3, Pallas kernels: none -> 47.1 us  [the longest x1 37.8 us: reduce_all(): pl.pallas_call(reduce_kernel, out_shape=jax.ShapeDtypeStruct((32, ROWS, 1...]
    unnamed x166 -> x14, local copies, waits for them, and re-layouts: 32.6 us -> 4.2 us
    dot_general x56 -> x0, matrix products: 25.8 us -> none  [the longest x27 18.3 us: block_section(): jnp.einsum('oc,bcv->bov', conv_weight[column], shifted_at(column), prefer...]
    gather x26 -> x0, local copies, waits for them, and re-layouts: 17 us -> none  [take_rows(): return jnp.take(extended, safe_index, axis=0)]
    slice x37 -> x1, local copies, waits for them, and re-layouts: 15.5 us -> 0.92 us  [body(): after = shift_strip(features[:, :, :128], -1)]
    concatenate x4 -> x0, other arithmetic: 12.1 us -> none  [the longest x2 10 us: build_padded(): return jnp.concatenate(layers, 2)]
    and x23 -> x0, other arithmetic: 8.5 us -> none  [take_rows(): return jnp.take(extended, safe_index, axis=0)]
  transfers between devices with their start and end apart: 3 -> 2, of which waited for: 1 -> 1; matrix products, arithmetic and copies ran while one was open for 8% -> 0% of each run, Pallas kernels for 0% -> 0%
where the time goes in v1:
time: 61.9 us; the launch traced here: 61.5 us
  Pallas kernels  47.1 us (76%)
  starting transfers between devices  7.53 us (12%)
  local copies, waits for them, and re-layouts  5.12 us (8%)
  between operations  1.38 us (2%)
    pallas_call x1, Pallas kernels, reduce_all(): pl.pallas_call(reduce_kernel, out_shape=jax.ShapeDtypeStruct((32, ROWS, 1...  37.8 us
    ppermute x2, starting transfers between devices, shift_strip(): return lax.ppermute(planes, 'space', route)  7.53 us
    pallas_call x1, Pallas kernels, local_math(): pl.pallas_call(local_kernel, out_shape=(jax.ShapeDtypeStruct((4, 64, 512)...  6.9 us
    unnamed x14, local copies, waits for them, and re-layouts  4.2 us
    pallas_call x1, Pallas kernels, unpack(): pl.pallas_call(unpack_kernel, out_shape=(jax.ShapeDtypeStruct((27, 64, 64...  2.4 us
  transfers between devices with their start and end apart: 2, of which 1 were waited for; matrix products, arithmetic and copies ran while one was open for 0% of the time, Pallas kernels for 0%

profile of v1, /device:TPU:1, one launch (start us, length us, event | category | flops | bytes accessed | tf_op | source)
XLA Modules:
  0.0 61.5 jit_solution(16721317961013986658)
XLA Ops:
  0.6 0.0 copy-start.5
  0.6 0.9 %fusion = (bf16[4,64,128]{2,1,0:T(8,128)(2,1)S(1)}, bf16[4,64,128]{2,1,0:T(8,128)(2,1)S(1)}) fusion(bf16[4,64,512]{2,1,0:T(8,128)(2,1)} %f_ref.1), kind=kLoop, calls=%fused_computation | loop fusion | bytes 262144 | tf_op jit(solution)/shard_map/slice | solution.py:350
  1.6 0.0 copy-start.1
  1.6 1.4 %collective-permute-start.1 = (bf16[4,64,128]{2,1,0:T(8,128)(2,1)S(1)}, bf16[4,64,128]{2,1,0:T(8,128)(2,1)S(1)}, u32[]{:S(2)}, u32[]{:S(2)}) collective-permute-start(bf16[4,64,128]{2,1,0:T(8,128)(2,1)S(1)} %get-tuple-element.14), channel_id=1, source_target_pairs={{4,0},{8,4},{12,8},{16,12},{20,16},{24,20},{28,24},{32,28},{36,32}... | collective-permute-start | bytes 196616 | tf_op jit(solution)/shard_map/ppermute | solution.py:345
  3.0 6.1 %collective-permute-start = (bf16[4,64,128]{2,1,0:T(8,128)(2,1)S(1)}, bf16[4,64,128]{2,1,0:T(8,128)(2,1)S(1)}, u32[]{:S(2)}, u32[]{:S(2)}) collective-permute-start(bf16[4,64,128]{2,1,0:T(8,128)(2,1)S(1)} %get-tuple-element.15), channel_id=1, source_target_pairs={{0,4},{4,8},{8,12},{12,16},{16,20},{20,24},{24,28},{28,32},{32,36}... | collective-permute-start | bytes 196616 | tf_op jit(solution)/shard_map/ppermute | solution.py:345
  9.8 0.0 copy-done.5
  9.8 0.0 copy-start.3
  9.8 0.0 copy-start.4
  9.8 0.2 copy.9.dw_ref
  10.0 0.0 collective-permute-done.1.next_ref
  10.0 0.4 collective-permute-done.prev_ref
  10.4 0.0 copy-done.1
  10.4 0.2 copy-done.3
  10.6 0.0 copy-done.4
  10.6 0.0 copy-start.2
  10.6 1.0 %copy-done.2 = bf16[27,64,64]{2,1,0:T(8,128)(2,1)S(1)} copy-done((bf16[27,64,64]{2,1,0:T(8,128)(2,1)S(1)}, bf16[27,64,64]{2,1,0:T(8,128)(2,1)}, u32[]{:S(2)}) %copy-start.2) | copy-done | bytes 221208
  11.6 6.9 %local_math.1 = (bf16[4,64,512]{2,1,0:T(8,128)(2,1)}, f32[32,48,128]{2,1,0:T(8,128)S(1)}) custom-call(s32[4,27]{1,0:T(4,128)S(1)} %copy-done.4, s32[1]{0:T(128)S(6)} %copy.11.cnt_ref, bf16[4,64,512]{2,1,0:T(8,128)(2,1)S(1)} %copy-done.1, bf16[4,64,128]{2,1,0:T(8,128)(2,1)S(1)} %collective-permute-done.prev_ref, ...), custom_call_target="tpu_custom_call" | custom-call | tf_op jit(solution)/shard_map/local_math/pallas_call | solution.py:171
  18.5 37.8 %reduce_all.1.v_ref = f32[32,48,128]{2,1,0:T(8,128)S(1)} custom-call(f32[32,48,128]{2,1,0:T(8,128)S(1)} %get-tuple-element.8.v_ref), custom_call_target="tpu_custom_call" | custom-call | tf_op jit(solution)/shard_map/reduce_all/pallas_call | solution.py:291
  56.3 0.0 copy-start
  56.3 0.9 %copy-done = f32[32,48,128]{2,1,0:T(8,128)} copy-done((f32[32,48,128]{2,1,0:T(8,128)}, f32[32,48,128]{2,1,0:T(8,128)S(1)}, u32[]{:S(2)}) %copy-start) | copy-done | bytes 786456
  57.2 2.4 %unpack.1 = (f32[27,64,64]{2,1,0:T(8,128)}, f32[8,128,64]{2,1,0:T(8,128)}) custom-call(f32[32,48,128]{2,1,0:T(8,128)} %copy-done), custom_call_target="tpu_custom_call" | custom-call | tf_op jit(solution)/shard_map/unpack/pallas_call | solution.py:330
  59.6 1.9 %copy.10 = f32[8,128,64]{1,2,0:T(8,128)} copy(f32[8,128,64]{2,1,0:T(8,128)} %get-tuple-element.13) | data formatting | bytes 524288
Async XLA Ops:
  0.6 9.1 %copy-start.5 = (bf16[8,128,64]{1,2,0:T(8,128)(2,1)S(1)}, bf16[8,128,64]{1,2,0:T(8,128)(2,1)}, u32[]{:S(2)}) copy-start(bf16[8,128,64]{1,2,0:T(8,128)(2,1)} %param.11) | copy-start | bytes 393220
  1.6 8.9 %copy-start.1 = (bf16[4,64,512]{2,1,0:T(8,128)(2,1)S(1)}, bf16[4,64,512]{2,1,0:T(8,128)(2,1)}, u32[]{:S(2)}) copy-start(bf16[4,64,512]{2,1,0:T(8,128)(2,1)} %f_ref.1) | copy-start | bytes 786436
  1.6 8.4 %collective-permute-start.1 = (bf16[4,64,128]{2,1,0:T(8,128)(2,1)S(1)}, bf16[4,64,128]{2,1,0:T(8,128)(2,1)S(1)}, u32[]{:S(2)}, u32[]{:S(2)}) collective-permute-start(bf16[4,64,128]{2,1,0:T(8,128)(2,1)S(1)} %get-tuple-element.14), channel_id=1, source_target_pairs={{4,0},{8,4},{12,8},{16,12},{20,16},{24,20},{28,24},{32,28},{36,32}... | collective-permute-start | bytes 196616 | tf_op jit(solution)/shard_map/ppermute | solution.py:345
  3.0 7.4 %collective-permute-start = (bf16[4,64,128]{2,1,0:T(8,128)(2,1)S(1)}, bf16[4,64,128]{2,1,0:T(8,128)(2,1)S(1)}, u32[]{:S(2)}, u32[]{:S(2)}) collective-permute-start(bf16[4,64,128]{2,1,0:T(8,128)(2,1)S(1)} %get-tuple-element.15), channel_id=1, source_target_pairs={{0,4},{4,8},{8,12},{12,16},{16,20},{20,24},{24,28},{28,32},{32,36}... | collective-permute-start | bytes 196616 | tf_op jit(solution)/shard_map/ppermute | solution.py:345
  9.8 0.8 %copy-start.3 = (bf16[4,64,128]{2,1,0:T(8,128)(2,1)S(1)}, bf16[4,64,128]{2,1,0:T(8,128)(2,1)}, u32[]{:S(2)}) copy-start(bf16[4,64,128]{2,1,0:T(8,128)(2,1)} %g_ref.1) | copy-start | bytes 196612
  9.8 0.8 %copy-start.4 = (s32[4,27]{1,0:T(4,128)S(1)}, s32[4,27]{1,0:T(4,128)}, u32[]{:S(2)}) copy-start(s32[4,27]{1,0:T(4,128)} %nb_ref.1) | copy-start | bytes 1300
  10.6 1.0 %copy-start.2 = (bf16[27,64,64]{2,1,0:T(8,128)(2,1)S(1)}, bf16[27,64,64]{2,1,0:T(8,128)(2,1)}, u32[]{:S(2)}) copy-start(bf16[27,64,64]{2,1,0:T(8,128)(2,1)} %cw_ref.1) | copy-start | bytes 663556
  56.3 0.9 %copy-start = (f32[32,48,128]{2,1,0:T(8,128)}, f32[32,48,128]{2,1,0:T(8,128)S(1)}, u32[]{:S(2)}) copy-start(f32[32,48,128]{2,1,0:T(8,128)S(1)} %reduce_all.1.v_ref) | copy-start | bytes 2359300

commit v2 on v1

v2 whole, which is shorter than its diff:
```python
import jax
import jax.numpy as jnp
from jax import lax
from jax.experimental import pallas as pl
from jax.experimental.pallas import tpu as pltpu
from jax.sharding import PartitionSpec as P

MESH = pl.DeviceIdType.MESH
F32, BF16 = jnp.float32, jnp.bfloat16
VM = pl.BlockSpec(memory_space=pltpu.VMEM)
SM = pl.BlockSpec(memory_space=pltpu.SMEM)
ANY = pl.BlockSpec(memory_space=pl.ANY)
HBM = pl.BlockSpec(memory_space=pltpu.HBM)
NX, NY, NZ = 4, 4, 8
NXY = NX * NY
CONV_ROWS, DOWN_ROWS = 32, 16
ROWS = CONV_ROWS + DOWN_ROWS


def dot(a, b, dims):
    return lax.dot_general(a, b, (dims, ((), ())), preferred_element_type=F32)


NN, NT, TN = ((1,), (0,)), ((1,), (1,)), ((0,), (0,))


def voxels_in_rows(block):
    wide = block.astype(F32)
    return jnp.concatenate([wide, wide], 0).T


def fill_weights(cw_ref, w_ref):
    for dy in range(3):
        for dx in range(3):
            row = [cw_ref[dx * 9 + dy * 3 + dz].astype(F32) for dz in range(3)]
            w_ref[dy, dx * 64 : dx * 64 + 64, :] = jnp.concatenate(row, 1).astype(BF16)


def fill_tables(f_ref, t_ref, lo_ref, hi_ref):
    for j in range(4):
        for q in range(4):
            part = voxels_in_rows(f_ref[j, :, q * 128 : q * 128 + 128])
            t_ref[j, q * 2 : q * 2 + 2] = part.reshape(2, 8, 8, 128)
        lo_ref[j] = t_ref[j, 7]
        hi_ref[j] = t_ref[j, 0]
    t_ref[4] = jnp.zeros((8, 8, 8, 128), F32)
    lo_ref[8] = jnp.zeros((8, 8, 128), F32)
    hi_ref[8] = jnp.zeros((8, 8, 128), F32)


def fill_halo(prev_ref, next_ref, lo_ref, hi_ref):
    for j in range(4):
        lo_ref[4 + j] = voxels_in_rows(prev_ref[j])[64:].reshape(8, 8, 128)
        hi_ref[4 + j] = voxels_in_rows(next_ref[j])[:64].reshape(8, 8, 128)


def store_plane(put, middle, below, above):
    z = lax.broadcasted_iota(jnp.int32, (10, 8, 128), 1)
    first = lax.broadcasted_iota(jnp.int32, (10, 8, 128), 2) < 64
    minus = pltpu.roll(jnp.where(z == 7, below, middle), 1, 1)
    plus = pltpu.roll(jnp.where(z == 0, above, middle), 7, 1)
    left = jnp.where(first, minus, middle)
    for dy in range(3):
        put(dy, 0, left[dy : dy + 8].reshape(64, 128).astype(BF16))
        put(dy, 128, plus[dy : dy + 8].reshape(64, 128).astype(BF16))


def link(nb_ref, b, ox, oy, oz, zero):
    j = nb_ref[b, (ox + 1) * 9 + (oy + 1) * 3 + oz + 1]
    return jnp.where(j < 0, zero, j)


def fill_inner(nb_ref, count, b, t_ref, q_ref):
    own = jnp.where(b < count, b, 4)
    idx = [[link(nb_ref, b, 0, oy, oz, 4) for oy in (-1, 0, 1)] for oz in (0, -1, 1)]
    idx[0][1] = own
    for xp in range(1, 9):
        cols = [
            jnp.concatenate(
                [t_ref[i0, xp - 1, 7:8], t_ref[i1, xp - 1], t_ref[i2, xp - 1, 0:1]], 0
            )
            for i0, i1, i2 in idx
        ]
        row = b * 512 + (xp - 1) * 64

        def put(dy, lane, rows, row=row):
            q_ref[dy, row : row + 64, lane : lane + 128] = rows

        store_plane(put, *cols)


def fill_outer(nb_ref, b, lo_ref, hi_ref, qo_ref):
    for ox, side, table in ((-1, 0, lo_ref), (1, 1, hi_ref)):
        cols = []
        for oz in (0, -1, 1):
            i0, i1, i2 = [link(nb_ref, b, ox, oy, oz, 8) for oy in (-1, 0, 1)]
            cols.append(jnp.concatenate([table[i0, 7:8], table[i1], table[i2, 0:1]], 0))

        def put(dy, lane, rows, side=side):
            qo_ref[dy, side, b * 64 : b * 64 + 64, lane : lane + 128] = rows

        store_plane(put, *cols)


def place_of(shape):
    v = lax.broadcasted_iota(jnp.int32, shape, 1)
    return (v // 64 % 2) * 4 + (v // 8 % 2) * 2 + v % 2


def cell_gradients(g_ref, dw_ref, count, b, up_ref, grad_ref):
    v = lax.broadcasted_iota(jnp.int32, (64, 512), 1)
    u = lax.broadcasted_iota(jnp.int32, (64, 512), 0)
    cell = (v // 128) * 16 + (v // 16 % 4) * 4 + v % 8 // 2
    spread = (cell == u).astype(F32).astype(BF16)
    grads = jnp.where(b < count, g_ref[b].astype(F32), 0.0)
    up = dot(grads.T.astype(BF16), spread, NN).astype(BF16)
    up_ref[:, b * 512 : b * 512 + 512] = up
    every = dot(dw_ref[...].reshape(512, 128), up, NN)
    place = place_of((64, 512))
    grad = every[0:64]
    for t in range(1, 8):
        grad = jnp.where(place == t, every[t * 64 : t * 64 + 64], grad)
    grad_ref[b] = grad


def inner_forward(b, w_ref, q_ref, pre_ref):
    acc = jnp.zeros((192, 512), F32)
    for dy in range(3):
        acc += dot(w_ref[dy], q_ref[dy, b * 512 : b * 512 + 512, 0:192], NT)
    gap = jnp.zeros((64, 64), F32)
    low = jnp.concatenate([gap, acc[0:64, 0:448]], 1)
    high = jnp.concatenate([acc[128:192, 64:512], gap], 1)
    pre_ref[b] = acc[64:128] + low + high


def outer_forward(w_ref, qo_ref):
    low, high = jnp.zeros((64, 256), F32), jnp.zeros((64, 256), F32)
    for dy in range(3):
        low += dot(w_ref[dy, 0:64], qo_ref[dy, 0, :, 0:192], NT)
        high += dot(w_ref[dy, 128:192], qo_ref[dy, 1, :, 0:192], NT)
    return low, high


def finish_block(b, low, high, pre_ref, grad_ref, hid_ref, hexp_ref, sh_ref):
    gap = jnp.zeros((64, 64), F32)
    wide = jnp.zeros((64, 384), F32)
    lanes = slice(b * 64, b * 64 + 64)
    pre = pre_ref[b] + jnp.concatenate([low[:, lanes], wide, high[:, lanes]], 1)
    hidden = jnp.maximum(pre, 0.0)
    hid_ref[b] = hidden.astype(BF16)
    place = place_of((64, 512))
    cols = slice(b * 512, b * 512 + 512)
    for t in range(8):
        hexp_ref[t * 64 : t * 64 + 64, cols] = jnp.where(place == t, hidden, 0.0).astype(BF16)
    act = jnp.where(pre > 0, grad_ref[b], 0.0)
    sh_ref[0:64, cols] = jnp.concatenate([act[:, 64:512], gap], 1).astype(BF16)
    sh_ref[64:128, cols] = act.astype(BF16)
    sh_ref[128:192, cols] = jnp.concatenate([gap, act[:, 0:448]], 1).astype(BF16)
    return act[:, 0:64], act[:, 448:512]


def put_rows(v_ref, at, rows):
    for i in range(0, rows.shape[0], CONV_ROWS):
        p = (at + i) // CONV_ROWS
        v_ref[p // NXY, p % NXY, 0:CONV_ROWS] = rows[i : i + CONV_ROWS]


def kernel_gradients(q_ref, qo_ref, sh_ref, lows, highs, up_ref, hexp_ref, v_ref):
    down = dot(hexp_ref[...], up_ref[...], NT)
    for p in range(2 * NXY):
        v_ref[p // NXY, p % NXY, CONV_ROWS:ROWS] = down[p * 16 : p * 16 + 16]
    low = jnp.concatenate(lows, 1).astype(BF16)
    high = jnp.concatenate(highs, 1).astype(BF16)
    plus = []
    for dy in range(3):
        grads = dot(sh_ref[...], q_ref[dy], NN)
        grads = jnp.concatenate(
            [
                grads[0:64] + dot(low, qo_ref[dy, 0], NN),
                grads[64:128],
                grads[128:192] + dot(high, qo_ref[dy, 1], NN),
            ],
            0,
        )
        put_rows(v_ref, dy * 192, grads[:, 0:128])
        plus.append(grads[:, 128:256])
    first = lax.broadcasted_iota(jnp.int32, (192, 128), 1) < 64
    put_rows(v_ref, 576, jnp.where(first, plus[0], plus[1]))
    put_rows(v_ref, 768, plus[2])
    put_rows(v_ref, 960, jnp.zeros((64, 128), F32))


def position():
    s, r = lax.axis_index("space"), lax.axis_index("rep")
    return s // 8, s // 2 % 4, s % 2 * 2 + r // 2, r % 2


def device(z, y, x, core):
    return {"space": z * 8 + y * 2 + x // 2, "rep": x % 2 * 2 + core}


def section_kernel(
    nb_ref, cnt_ref, f_hbm, g_hbm, cw_hbm, dw_hbm, hid_hbm, o_ref,
    f_ref, g_ref, cw_ref, dw_ref, prev_ref, next_ref, t_ref, lo_ref, hi_ref, q_ref, qo_ref, w_ref,
    up_ref, grad_ref, pre_ref, hid_ref, hexp_ref, sh_ref,
    v_ref, mate, outgoing, parts, along, ls, hs, hr, ss, rs, zs, zr, gs, gr, cs, cr,
):
    z, y, x, core = position()
    me = y * NX + x
    sibling = device(z, y, x, 1 - core)
    plane = [(dy, dx) for dy in range(NY) for dx in range(NX) if dy or dx]
    plane.sort(key=lambda o: -(min(o[0], NY - o[0]) + min(o[1], NX - o[1])))

    def plane_peer(o):
        py, px = (y + o[0]) % NY, (x + o[1]) % NX
        return device(z, py, px, core), py * NX + px

    def line_peer(dz):
        return device((z + dz) % NZ, y, x, core)

    strip, tile = lax.axis_index("space"), lax.axis_index("rep")
    strips = NX // 2 * NY * NZ
    above = {"space": (strip + 1) % strips, "rep": tile}
    below = {"space": (strip + strips - 1) % strips, "rep": tile}

    barrier = pltpu.get_barrier_semaphore()
    greet = [above, below] + [plane_peer(o)[0] for o in plane] + [line_peer(d) for d in range(1, NZ)]
    greet.append(sibling)
    for d in greet:
        pl.semaphore_signal(barrier, inc=1, device_id=d, device_id_type=MESH)
    loads = [
        pltpu.make_async_copy(src, dst, ls.at[i])
        for i, (src, dst) in enumerate(
            ((f_hbm, f_ref), (cw_hbm, cw_ref), (g_hbm, g_ref), (dw_hbm, dw_ref))
        )
    ]
    for c in loads:
        c.start()
    count = cnt_ref[0]

    loads[0].wait()
    fill_tables(f_ref, t_ref, lo_ref, hi_ref)
    pl.semaphore_wait(barrier, len(greet))
    halo = [
        pltpu.make_async_remote_copy(
            f_ref.at[:, :, pl.ds(384, 128)], prev_ref, hs.at[0], hr.at[0],
            device_id=above, device_id_type=MESH,
        ),
        pltpu.make_async_remote_copy(
            f_ref.at[:, :, pl.ds(0, 128)], next_ref, hs.at[1], hr.at[1],
            device_id=below, device_id_type=MESH,
        ),
    ]
    for c in halo:
        c.start()
    loads[1].wait()
    fill_weights(cw_ref, w_ref)
    loads[2].wait()
    loads[3].wait()
    for b in range(4):
        fill_inner(nb_ref, count, b, t_ref, q_ref)
        cell_gradients(g_ref, dw_ref, count, b, up_ref, grad_ref)
        inner_forward(b, w_ref, q_ref, pre_ref)

    for c in halo:
        c.wait()
    fill_halo(prev_ref, next_ref, lo_ref, hi_ref)
    for b in range(4):
        fill_outer(nb_ref, b, lo_ref, hi_ref, qo_ref)
    low, high = outer_forward(w_ref, qo_ref)
    ends = [
        finish_block(b, low, high, pre_ref, grad_ref, hid_ref, hexp_ref, sh_ref)
        for b in range(4)
    ]
    hidden_out = pltpu.make_async_copy(hid_ref, hid_hbm, ls.at[4])
    hidden_out.start()
    kernel_gradients(
        q_ref, qo_ref, sh_ref, [e[0] for e in ends], [e[1] for e in ends], up_ref, hexp_ref, v_ref
    )

    order = [plane_peer(o) for o in plane]
    halves = []
    for i, at in enumerate([at for _, at in order] + [me]):
        halves.append(
            pltpu.make_async_remote_copy(
                v_ref.at[1 - core, at], mate.at[at], cs.at[i], cr.at[i],
                device_id=sibling, device_id_type=MESH,
            )
        )
        halves[-1].start()
    copies = []
    for i, (peer, at) in enumerate(order):
        halves[i].wait_recv()
        outgoing[i] = (v_ref[core, at] + mate[at]).astype(BF16)
        copies.append(
            pltpu.make_async_remote_copy(
                outgoing.at[i], parts.at[i], ss.at[i], rs.at[i],
                device_id=peer, device_id_type=MESH,
            )
        )
        copies[-1].start()
    halves[-1].wait_recv()
    total = v_ref[core, me] + mate[me]
    for i, c in enumerate(copies):
        c.wait_recv()
        total = total + parts[i].astype(F32)

    along[z] = total.astype(BF16)
    lines = []
    for i, dz in enumerate((4, 3, 5, 2, 6, 1, 7)):
        lines.append(
            pltpu.make_async_remote_copy(
                along.at[z], along.at[z], zs.at[i], zr.at[i],
                device_id=line_peer(dz), device_id_type=MESH,
            )
        )
        lines[-1].start()
    for c in halves + copies:
        c.wait_send()
    for c in lines:
        c.wait_recv()
    total = along[0].astype(F32)
    for i in range(1, NZ):
        total = total + along[i].astype(F32)

    half = core * NXY
    o_ref[half + me] = total
    last = []
    for i, (peer, _) in enumerate(order):
        last.append(
            pltpu.make_async_remote_copy(
                o_ref.at[half + me], o_ref.at[half + me], gs.at[i], gr.at[i],
                device_id=peer, device_id_type=MESH,
            )
        )
        last[-1].start()
    for c in lines:
        c.wait_send()
    for c in last:
        c.wait()
    rest = pltpu.make_async_remote_copy(
        o_ref.at[pl.ds(half, NXY)], o_ref.at[pl.ds(half, NXY)], cs.at[NXY], cr.at[NXY],
        device_id=sibling, device_id_type=MESH,
    )
    rest.start()
    rest.wait()
    hidden_out.wait()


def section(features, neighbours, counts, cotangent, conv_weight, down_weight):
    dma = pltpu.SemaphoreType.DMA
    vm = pltpu.VMEM
    near, line = NXY - 1, NZ - 1
    return pl.pallas_call(
        section_kernel,
        out_shape=(
            jax.ShapeDtypeStruct((4, 64, 512), BF16),
            jax.ShapeDtypeStruct((32, ROWS, 128), F32),
        ),
        in_specs=[SM, SM, HBM, HBM, HBM, HBM],
        out_specs=(ANY, VM),
        scratch_shapes=[
            vm((4, 64, 512), BF16), vm((4, 64, 128), BF16), vm((27, 64, 64), BF16), vm((8, 64, 128), BF16),
            vm((4, 64, 128), BF16), vm((4, 64, 128), BF16),
            vm((5, 8, 8, 8, 128), F32), vm((9, 8, 8, 128), F32), vm((9, 8, 8, 128), F32),
            vm((3, 2048, 256), BF16), vm((3, 2, 256, 256), BF16), vm((3, 192, 192), BF16),
            vm((128, 2048), BF16), vm((4, 64, 512), F32), vm((4, 64, 512), F32), vm((4, 64, 512), BF16),
            vm((512, 2048), BF16), vm((192, 2048), BF16),
            vm((2, NXY, ROWS, 128), F32), vm((NXY, ROWS, 128), F32),
            vm((near, ROWS, 128), BF16), vm((near, ROWS, 128), BF16), vm((NZ, ROWS, 128), BF16),
            dma((5,)), dma((2,)), dma((2,)), dma((near,)), dma((near,)), dma((line,)), dma((line,)),
            dma((near,)), dma((near,)), dma((NXY + 1,)), dma((NXY + 1,)),
        ],
        compiler_params=pltpu.CompilerParams(
            collective_id=0, has_side_effects=True, vmem_limit_bytes=48 << 20
        ),
        name="section",
    )(neighbours, counts, features, cotangent, conv_weight, down_weight)


def unpack_kernel(v_ref, hid_hbm, conv_ref, down_ref, out_hbm, sem):
    through = pltpu.make_async_copy(hid_hbm, out_hbm, sem)
    through.start()
    conv = v_ref[:, 0:CONV_ROWS].reshape(1024, 128)
    for dy in range(3):
        for dx in range(3):
            at = dy * 192 + dx * 64
            pair = conv[at : at + 64]
            conv_ref[dx * 9 + dy * 3] = pair[:, 0:64]
            conv_ref[dx * 9 + dy * 3 + 1] = pair[:, 64:128]
            at = 768 + dx * 64 if dy == 2 else 576 + dx * 64
            side = 64 if dy == 1 else 0
            conv_ref[dx * 9 + dy * 3 + 2] = conv[at : at + 64, side : side + 64]
    down_ref[...] = v_ref[:, CONV_ROWS:ROWS].reshape(8, 64, 128)
    through.wait()


def unpack(pieces, hidden):
    return pl.pallas_call(
        unpack_kernel,
        out_shape=(
            jax.ShapeDtypeStruct((27, 64, 64), F32),
            jax.ShapeDtypeStruct((8, 64, 128), F32),
            jax.ShapeDtypeStruct((4, 64, 512), BF16),
        ),
        in_specs=[VM, ANY],
        out_specs=(VM, VM, ANY),
        scratch_shapes=[pltpu.SemaphoreType.DMA],
        compiler_params=pltpu.CompilerParams(vmem_limit_bytes=16 << 20),
        name="unpack",
    )(pieces, hidden)


def body(features, neighbours, counts, cotangent, conv_weight, down_weight):
    down_rows = jnp.swapaxes(down_weight, 1, 2)
    hidden, pieces = section(features, neighbours, counts, cotangent, conv_weight, down_rows)
    conv_grad, down_grad, hidden = unpack(pieces, hidden)
    return hidden, conv_grad, jnp.swapaxes(down_grad, 1, 2)


def solution(mesh):
    both = ("space", "rep")
    return jax.shard_map(
        body,
        mesh=mesh,
        in_specs=(
            P(both, None, None), P(both, None), P(both), P(both, None, None), P(), P(),
        ),
        out_specs=(P(both, None, None), P(), P()),
        check_vma=False,
    )
```

time: 61.9 us -> 47.3 us (0.76)
  starting transfers between devices: 7.53 us -> 0 us
  Pallas kernels: 47.1 us -> 42.1 us
  local copies, waits for them, and re-layouts: 5.12 us -> 3.72 us
    ppermute x2 -> x0, starting transfers between devices: 7.53 us -> none  [shift_strip(): return lax.ppermute(planes, 'space', route)]
    pallas_call x2 -> x1, Pallas kernels: 44.7 us -> 40.3 us  [section(): pl.pallas_call(section_kernel, out_shape=(jax.ShapeDtypeStruct((4, 64, 51...]
    slice x1 -> x0, local copies, waits for them, and re-layouts: 0.92 us -> none  [body(): after = shift_strip(features[:, :, :128], -1)]
    pallas_call x1, Pallas kernels: 2.4 us -> 1.73 us  [unpack(): pl.pallas_call(unpack_kernel, out_shape=(jax.ShapeDtypeStruct((27, 64, 64...]
    unnamed x14 -> x10, local copies, waits for them, and re-layouts: 4.2 us -> 3.72 us
  transfers between devices with their start and end apart: 2 -> 0, of which waited for: 1 -> 0; matrix products, arithmetic and copies ran while one was open for 0% -> 0% of each run, Pallas kernels for 0% -> 0%
where the time goes in v2:
time: 47.3 us; the launch traced here: 47.1 us
  Pallas kernels  42.1 us (89%)
  local copies, waits for them, and re-layouts  3.72 us (8%)
  between operations  1.31 us (3%)
    pallas_call x1, Pallas kernels, section(): pl.pallas_call(section_kernel, out_shape=(jax.ShapeDtypeStruct((4, 64, 51...  40.3 us
    unnamed x10, local copies, waits for them, and re-layouts  3.72 us
    pallas_call x1, Pallas kernels, unpack(): pl.pallas_call(unpack_kernel, out_shape=(jax.ShapeDtypeStruct((27, 64, 64...  1.73 us

profile of v2, /device:TPU:1, one launch (start us, length us, event | category | flops | bytes accessed | tf_op | source)
XLA Modules:
  0.0 47.1 jit_solution(12312875475213610754)
XLA Ops:
  0.6 0.0 copy-start.4
  1.3 0.0 copy-done.4
  1.3 0.0 copy-start
  1.3 1.0 %copy-done = bf16[27,64,64]{2,1,0:T(8,128)(2,1)S(1)} copy-done((bf16[27,64,64]{2,1,0:T(8,128)(2,1)S(1)}, bf16[27,64,64]{2,1,0:T(8,128)(2,1)}, u32[]{:S(2)}) %copy-start) | copy-done | bytes 221208
  2.3 0.0 copy-start.1
  2.3 0.9 %copy-done.1 = bf16[4,64,512]{2,1,0:T(8,128)(2,1)S(1)} copy-done((bf16[4,64,512]{2,1,0:T(8,128)(2,1)S(1)}, bf16[4,64,512]{2,1,0:T(8,128)(2,1)}, u32[]{:S(2)}) %copy-start.1) | copy-done | bytes 262168
  3.3 0.0 copy-start.2
  3.3 0.9 %copy-done.2 = bf16[8,128,64]{1,2,0:T(8,128)(2,1)S(1)} copy-done((bf16[8,128,64]{1,2,0:T(8,128)(2,1)S(1)}, bf16[8,128,64]{1,2,0:T(8,128)(2,1)}, u32[]{:S(2)}) %copy-start.2) | copy-done | bytes 131096
  4.2 0.0 copy-start.3
  4.2 0.8 %copy-done.3 = bf16[4,64,128]{2,1,0:T(8,128)(2,1)S(1)} copy-done((bf16[4,64,128]{2,1,0:T(8,128)(2,1)S(1)}, bf16[4,64,128]{2,1,0:T(8,128)(2,1)}, u32[]{:S(2)}) %copy-start.3) | copy-done | bytes 65560
  5.0 40.3 %section.1 = (bf16[4,64,512]{2,1,0:T(8,128)(2,1)S(1)}, f32[32,48,128]{2,1,0:T(8,128)S(1)}) custom-call(s32[4,27]{1,0:T(4,128)S(1)} %copy-done.4, s32[1]{0:T(128)S(6)} %copy.9.cnt_ref, bf16[4,64,512]{2,1,0:T(8,128)(2,1)S(1)} %copy-done.1, bf16[4,64,128]{2,1,0:T(8,128)(2,1)S(1)} %copy-done.3, bf16[27,64,64]{2,1,0:T(8,128)(2,1)S(1)} %copy-done, ...), custom_call_target="tpu_custom_call" | custom-call | tf_op jit(solution)/shard_map/section/pallas_call | solution.py:354
  45.4 1.7 %unpack.1 = (f32[27,64,64]{2,1,0:T(8,128)}, f32[8,64,128]{2,1,0:T(8,128)}, bf16[4,64,512]{2,1,0:T(8,128)(2,1)}) custom-call(f32[32,48,128]{2,1,0:T(8,128)S(1)} %get-tuple-element.8.v_ref, bf16[4,64,512]{2,1,0:T(8,128)(2,1)S(1)} %get-tuple-element.9.hid_hbm), custom_call_target="tpu_custom_call" | custom-call | tf_op jit(solution)/shard_map/unpack/pallas_call | solution.py:399
Async XLA Ops:
  0.6 0.7 %copy-start.4 = (s32[4,27]{1,0:T(4,128)S(1)}, s32[4,27]{1,0:T(4,128)}, u32[]{:S(2)}) copy-start(s32[4,27]{1,0:T(4,128)} %nb_ref.1) | copy-start | bytes 1300
  1.3 1.0 %copy-start = (bf16[27,64,64]{2,1,0:T(8,128)(2,1)S(1)}, bf16[27,64,64]{2,1,0:T(8,128)(2,1)}, u32[]{:S(2)}) copy-start(bf16[27,64,64]{2,1,0:T(8,128)(2,1)} %cw_hbm.1) | copy-start | bytes 663556
  2.3 0.9 %copy-start.1 = (bf16[4,64,512]{2,1,0:T(8,128)(2,1)S(1)}, bf16[4,64,512]{2,1,0:T(8,128)(2,1)}, u32[]{:S(2)}) copy-start(bf16[4,64,512]{2,1,0:T(8,128)(2,1)} %f_hbm.1) | copy-start | bytes 786436
  3.3 0.9 %copy-start.2 = (bf16[8,128,64]{1,2,0:T(8,128)(2,1)S(1)}, bf16[8,128,64]{1,2,0:T(8,128)(2,1)}, u32[]{:S(2)}) copy-start(bf16[8,128,64]{1,2,0:T(8,128)(2,1)} %param.11) | copy-start | bytes 393220
  4.2 0.8 %copy-start.3 = (bf16[4,64,128]{2,1,0:T(8,128)(2,1)S(1)}, bf16[4,64,128]{2,1,0:T(8,128)(2,1)}, u32[]{:S(2)}) copy-start(bf16[4,64,128]{2,1,0:T(8,128)(2,1)} %g_hbm.1) | copy-start | bytes 196612

commit v3 on v2

--- a/solution.py
+++ b/solution.py
@@ -10,7 +10,6 @@
 VM = pl.BlockSpec(memory_space=pltpu.VMEM)
 SM = pl.BlockSpec(memory_space=pltpu.SMEM)
 ANY = pl.BlockSpec(memory_space=pl.ANY)
-HBM = pl.BlockSpec(memory_space=pltpu.HBM)
 NX, NY, NZ = 4, 4, 8
 NXY = NX * NY
 CONV_ROWS, DOWN_ROWS = 32, 16
@@ -200,9 +199,9 @@
 
 
 def section_kernel(
-    nb_ref, cnt_ref, f_hbm, g_hbm, cw_hbm, dw_hbm, hid_hbm, o_ref,
+    nb_ref, cnt_ref, f_hbm, g_hbm, cw_hbm, dw_hbm, hid_ref, o_ref,
     f_ref, g_ref, cw_ref, dw_ref, prev_ref, next_ref, t_ref, lo_ref, hi_ref, q_ref, qo_ref, w_ref,
-    up_ref, grad_ref, pre_ref, hid_ref, hexp_ref, sh_ref,
+    up_ref, grad_ref, pre_ref, hexp_ref, sh_ref,
     v_ref, mate, outgoing, parts, along, ls, hs, hr, ss, rs, zs, zr, gs, gr, cs, cr,
 ):
     z, y, x, core = position()
@@ -223,19 +222,19 @@
     above = {"space": (strip + 1) % strips, "rep": tile}
     below = {"space": (strip + strips - 1) % strips, "rep": tile}
 
+    loads = [
+        pltpu.make_async_copy(src, dst, ls.at[i])
+        for i, (src, dst) in enumerate(
+            ((f_hbm, f_ref), (cw_hbm, cw_ref), (g_hbm, g_ref), (dw_hbm, dw_ref))
+        )
+    ]
+    for c in loads:
+        c.start()
     barrier = pltpu.get_barrier_semaphore()
     greet = [above, below] + [plane_peer(o)[0] for o in plane] + [line_peer(d) for d in range(1, NZ)]
     greet.append(sibling)
     for d in greet:
         pl.semaphore_signal(barrier, inc=1, device_id=d, device_id_type=MESH)
-    loads = [
-        pltpu.make_async_copy(src, dst, ls.at[i])
-        for i, (src, dst) in enumerate(
-            ((f_hbm, f_ref), (cw_hbm, cw_ref), (g_hbm, g_ref), (dw_hbm, dw_ref))
-        )
-    ]
-    for c in loads:
-        c.start()
     count = cnt_ref[0]
 
     loads[0].wait()
@@ -272,8 +271,6 @@
         finish_block(b, low, high, pre_ref, grad_ref, hid_ref, hexp_ref, sh_ref)
         for b in range(4)
     ]
-    hidden_out = pltpu.make_async_copy(hid_ref, hid_hbm, ls.at[4])
-    hidden_out.start()
     kernel_gradients(
         q_ref, qo_ref, sh_ref, [e[0] for e in ends], [e[1] for e in ends], up_ref, hexp_ref, v_ref
     )
@@ -344,7 +341,6 @@
     )
     rest.start()
     rest.wait()
-    hidden_out.wait()
 
 
 def section(features, neighbours, counts, cotangent, conv_weight, down_weight):
@@ -354,36 +350,40 @@
     return pl.pallas_call(
         section_kernel,
         out_shape=(
-            jax.ShapeDtypeStruct((4, 64, 512), BF16),
-            jax.ShapeDtypeStruct((32, ROWS, 128), F32),
-        ),
-        in_specs=[SM, SM, HBM, HBM, HBM, HBM],
-        out_specs=(ANY, VM),
+            pltpu.VMEM((4, 64, 512), BF16),
+            pltpu.VMEM((32, ROWS, 128), F32),
+        ),
+        in_specs=[SM, SM, ANY, ANY, ANY, ANY],
+        out_specs=(VM, VM),
         scratch_shapes=[
             vm((4, 64, 512), BF16), vm((4, 64, 128), BF16), vm((27, 64, 64), BF16), vm((8, 64, 128), BF16),
             vm((4, 64, 128), BF16), vm((4, 64, 128), BF16),
             vm((5, 8, 8, 8, 128), F32), vm((9, 8, 8, 128), F32), vm((9, 8, 8, 128), F32),
             vm((3, 2048, 256), BF16), vm((3, 2, 256, 256), BF16), vm((3, 192, 192), BF16),
-            vm((128, 2048), BF16), vm((4, 64, 512), F32), vm((4, 64, 512), F32), vm((4, 64, 512), BF16),
+            vm((128, 2048), BF16), vm((4, 64, 512), F32), vm((4, 64, 512), F32),
             vm((512, 2048), BF16), vm((192, 2048), BF16),
             vm((2, NXY, ROWS, 128), F32), vm((NXY, ROWS, 128), F32),
             vm((near, ROWS, 128), BF16), vm((near, ROWS, 128), BF16), vm((NZ, ROWS, 128), BF16),
-            dma((5,)), dma((2,)), dma((2,)), dma((near,)), dma((near,)), dma((line,)), dma((line,)),
+            dma((4,)), dma((2,)), dma((2,)), dma((near,)), dma((near,)), dma((line,)), dma((line,)),
             dma((near,)), dma((near,)), dma((NXY + 1,)), dma((NXY + 1,)),
         ],
         compiler_params=pltpu.CompilerParams(
-            collective_id=0, has_side_effects=True, vmem_limit_bytes=48 << 20
+            collective_id=0, has_side_effects=True, vmem_limit_bytes=56 << 20
         ),
         name="section",
     )(neighbours, counts, features, cotangent, conv_weight, down_weight)
 
 
-def unpack_kernel(v_ref, hid_hbm, conv_ref, down_ref, out_hbm, sem):
-    through = pltpu.make_async_copy(hid_hbm, out_hbm, sem)
-    through.start()
+def unpack_kernel(v_ref, hid_ref, conv_hbm, down_hbm, hid_hbm, conv_ref, sem):
+    moves = [
+        pltpu.make_async_copy(v_ref.at[:, pl.ds(CONV_ROWS, DOWN_ROWS), :], down_hbm, sem.at[0]),
+        pltpu.make_async_copy(hid_ref, hid_hbm, sem.at[1]),
+    ]
+    for m in moves:
+        m.start()
     conv = v_ref[:, 0:CONV_ROWS].reshape(1024, 128)
-    for dy in range(3):
-        for dx in range(3):
+    for dx in range(3):
+        for dy in range(3):
             at = dy * 192 + dx * 64
             pair = conv[at : at + 64]
             conv_ref[dx * 9 + dy * 3] = pair[:, 0:64]
@@ -391,8 +391,13 @@
             at = 768 + dx * 64 if dy == 2 else 576 + dx * 64
             side = 64 if dy == 1 else 0
             conv_ref[dx * 9 + dy * 3 + 2] = conv[at : at + 64, side : side + 64]
-    down_ref[...] = v_ref[:, CONV_ROWS:ROWS].reshape(8, 64, 128)
-    through.wait()
+        part = pl.ds(dx * 9, 9)
+        moves.append(
+            pltpu.make_async_copy(conv_ref.at[part], conv_hbm.at[part], sem.at[2 + dx])
+        )
+        moves[-1].start()
+    for m in moves:
+        m.wait()
 
 
 def unpack(pieces, hidden):
@@ -400,13 +405,13 @@
         unpack_kernel,
         out_shape=(
             jax.ShapeDtypeStruct((27, 64, 64), F32),
-            jax.ShapeDtypeStruct((8, 64, 128), F32),
+            jax.ShapeDtypeStruct((32, DOWN_ROWS, 128), F32),
             jax.ShapeDtypeStruct((4, 64, 512), BF16),
         ),
-        in_specs=[VM, ANY],
-        out_specs=(VM, VM, ANY),
-        scratch_shapes=[pltpu.SemaphoreType.DMA],
-        compiler_params=pltpu.CompilerParams(vmem_limit_bytes=16 << 20),
+        in_specs=[VM, VM],
+        out_specs=(ANY, ANY, ANY),
+        scratch_shapes=[pltpu.VMEM((27, 64, 64), F32), pltpu.SemaphoreType.DMA((5,))],
+        compiler_params=pltpu.CompilerParams(vmem_limit_bytes=48 << 20),
         name="unpack",
     )(pieces, hidden)
 
@@ -415,7 +420,7 @@
     down_rows = jnp.swapaxes(down_weight, 1, 2)
     hidden, pieces = section(features, neighbours, counts, cotangent, conv_weight, down_rows)
     conv_grad, down_grad, hidden = unpack(pieces, hidden)
-    return hidden, conv_grad, jnp.swapaxes(down_grad, 1, 2)
+    return hidden, conv_grad, jnp.swapaxes(down_grad.reshape(8, 64, 128), 1, 2)
 
 
 def solution(mesh):

time: 47.3 us -> 42.5 us (0.90)
  local copies, waits for them, and re-layouts: 3.72 us -> 0 us
  Pallas kernels: 42.1 us -> 41.1 us
    unnamed x10 -> x0, local copies, waits for them, and re-layouts: 3.72 us -> none
    pallas_call x1, Pallas kernels: 1.73 us -> 1.13 us  [unpack(): pl.pallas_call(unpack_kernel, out_shape=(jax.ShapeDtypeStruct((27, 64, 64...]
where the time goes in v3:
time: 42.5 us; the launch traced here: 42.4 us
  Pallas kernels  41.1 us (97%)
  between operations  1.29 us (3%)
    pallas_call x1, Pallas kernels, section(): pl.pallas_call(section_kernel, out_shape=(pltpu.VMEM((4, 64, 512), BF16),...  40 us
    pallas_call x1, Pallas kernels, unpack(): pl.pallas_call(unpack_kernel, out_shape=(jax.ShapeDtypeStruct((27, 64, 64...  1.13 us

profile of v3, /device:TPU:1, one launch (start us, length us, event | category | flops | bytes accessed | tf_op | source)
XLA Modules:
  0.0 42.4 jit_solution(9196076725446940572)
XLA Ops:
  1.3 40.0 %section.1 = (bf16[4,64,512]{2,1,0:T(8,128)(2,1)S(1)}, f32[32,48,128]{2,1,0:T(8,128)S(1)}) custom-call(s32[4,27]{1,0:T(4,128)} %nb_ref.1, s32[1]{0:T(128)S(6)} %copy.9.cnt_ref, bf16[4,64,512]{2,1,0:T(8,128)(2,1)} %f_hbm.1, bf16[4,64,128]{2,1,0:T(8,128)(2,1)} %g_hbm.1, bf16[27,64,64]{2,1,0:T(8,128)(2,1)} %cw_hbm.1, bf16[8,64,128]{2,1,0:T(8,128)(2,1)} %bitcast.4), custom_call_target="tpu_custom_call" | custom-call | tf_op jit(solution)/shard_map/section/pallas_call | solution.py:350
  41.3 1.1 %unpack.1 = (f32[27,64,64]{2,1,0:T(8,128)}, f32[32,16,128]{2,1,0:T(8,128)}, bf16[4,64,512]{2,1,0:T(8,128)(2,1)}) custom-call(f32[32,48,128]{2,1,0:T(8,128)S(1)} %get-tuple-element.8.v_ref, bf16[4,64,512]{2,1,0:T(8,128)(2,1)S(1)} %get-tuple-element.9.hid_ref), custom_call_target="tpu_custom_call" | custom-call | tf_op jit(solution)/shard_map/unpack/pallas_call | solution.py:404

commit v4 on v3

--- a/solution.py
+++ b/solution.py
@@ -69,7 +69,7 @@
     return jnp.where(j < 0, zero, j)
 
 
-def fill_inner(nb_ref, count, b, t_ref, q_ref):
+def fill_inner(nb_ref, count, b, t_ref, q_ref, qe_ref):
     own = jnp.where(b < count, b, 4)
     idx = [[link(nb_ref, b, 0, oy, oz, 4) for oy in (-1, 0, 1)] for oz in (0, -1, 1)]
     idx[0][1] = own
@@ -80,23 +80,29 @@
             )
             for i0, i1, i2 in idx
         ]
-        row = b * 512 + (xp - 1) * 64
-
-        def put(dy, lane, rows, row=row):
+        row, edge = b * 512 + (xp - 1) * 64, b * 64
+
+        def put(dy, lane, rows, row=row, edge=edge, xp=xp):
             q_ref[dy, row : row + 64, lane : lane + 128] = rows
+            if xp in (1, 2):
+                qe_ref[dy, xp, edge : edge + 64, lane : lane + 128] = rows
+            if xp in (7, 8):
+                qe_ref[dy, xp - 7, 256 + edge : 320 + edge, lane : lane + 128] = rows
 
         store_plane(put, *cols)
 
 
-def fill_outer(nb_ref, b, lo_ref, hi_ref, qo_ref):
+def fill_outer(nb_ref, b, lo_ref, hi_ref, qe_ref):
     for ox, side, table in ((-1, 0, lo_ref), (1, 1, hi_ref)):
         cols = []
         for oz in (0, -1, 1):
             i0, i1, i2 = [link(nb_ref, b, ox, oy, oz, 8) for oy in (-1, 0, 1)]
             cols.append(jnp.concatenate([table[i0, 7:8], table[i1], table[i2, 0:1]], 0))
 
-        def put(dy, lane, rows, side=side):
-            qo_ref[dy, side, b * 64 : b * 64 + 64, lane : lane + 128] = rows
+        row = side * 256 + b * 64
+
+        def put(dy, lane, rows, side=side, row=row):
+            qe_ref[dy, 2 * side, row : row + 64, lane : lane + 128] = rows
 
         store_plane(put, *cols)
 
@@ -132,19 +138,19 @@
     pre_ref[b] = acc[64:128] + low + high
 
 
-def outer_forward(w_ref, qo_ref):
+def outer_forward(w_ref, qe_ref):
     low, high = jnp.zeros((64, 256), F32), jnp.zeros((64, 256), F32)
     for dy in range(3):
-        low += dot(w_ref[dy, 0:64], qo_ref[dy, 0, :, 0:192], NT)
-        high += dot(w_ref[dy, 128:192], qo_ref[dy, 1, :, 0:192], NT)
+        low += dot(w_ref[dy, 0:64], qe_ref[dy, 0, 0:256, 0:192], NT)
+        high += dot(w_ref[dy, 128:192], qe_ref[dy, 2, 256:512, 0:192], NT)
     return low, high
 
 
-def finish_block(b, low, high, pre_ref, grad_ref, hid_ref, hexp_ref, sh_ref):
+def inner_block(b, pre_ref, grad_ref, hid_ref, hexp_ref, sh_ref):
+    lane = lax.broadcasted_iota(jnp.int32, (64, 512), 1)
+    inside = (lane >= 64) & (lane < 448)
     gap = jnp.zeros((64, 64), F32)
-    wide = jnp.zeros((64, 384), F32)
-    lanes = slice(b * 64, b * 64 + 64)
-    pre = pre_ref[b] + jnp.concatenate([low[:, lanes], wide, high[:, lanes]], 1)
+    pre = jnp.where(inside, pre_ref[b], 0.0)
     hidden = jnp.maximum(pre, 0.0)
     hid_ref[b] = hidden.astype(BF16)
     place = place_of((64, 512))
@@ -155,72 +161,103 @@
     sh_ref[0:64, cols] = jnp.concatenate([act[:, 64:512], gap], 1).astype(BF16)
     sh_ref[64:128, cols] = act.astype(BF16)
     sh_ref[128:192, cols] = jnp.concatenate([gap, act[:, 0:448]], 1).astype(BF16)
-    return act[:, 0:64], act[:, 448:512]
+
+
+def edge_lanes(side):
+    return slice(448, 512) if side else slice(0, 64)
+
+
+def stash_edges(pre_ref, grad_ref, up_ref, pe_ref, ge_ref, ue_ref):
+    for side in range(2):
+        at = edge_lanes(side)
+        pe_ref[side] = jnp.concatenate([pre_ref[b, :, at] for b in range(4)], 1)
+        ge_ref[side] = jnp.concatenate([grad_ref[b, :, at] for b in range(4)], 1)
+        ups = [up_ref[:, b * 512 + at.start : b * 512 + at.stop].astype(F32) for b in range(4)]
+        ue_ref[side] = jnp.concatenate(ups, 1).astype(BF16)
+
+
+def edge_planes(sums, pe_ref, ge_ref, ue_ref, hid_ref, dg_ref, down_ref):
+    v = lax.broadcasted_iota(jnp.int32, (64, 256), 1)
+    place = (v // 8 % 2) * 2 + v % 2
+    first = lax.broadcasted_iota(jnp.int32, (64, 128), 1) < 64
+    acts = []
+    for side in range(2):
+        pre = pe_ref[side] + sums[side]
+        hidden = jnp.maximum(pre, 0.0)
+        acts.append(jnp.where(pre > 0, ge_ref[side], 0.0))
+        spread = jnp.concatenate([jnp.where(place == t, hidden, 0.0) for t in range(4)], 0)
+        down = dg_ref[side * 256 : side * 256 + 256] + dot(spread.astype(BF16), ue_ref[side], NT)
+        for p in range(NXY):
+            down_ref[side, p] = down[p * 16 : p * 16 + 16]
+        tile = slice(384, 512) if side else slice(0, 128)
+        for b in range(4):
+            mine = hidden[:, b // 2 * 128 : b // 2 * 128 + 128]
+            if b % 2 != side:
+                mine = pltpu.roll(mine, 64, 1)
+            old = hid_ref[b, :, tile].astype(F32)
+            hid_ref[b, :, tile] = jnp.where(first != (side == 1), mine, old).astype(BF16)
+    return jnp.concatenate(acts, 1).astype(BF16)
 
 
 def put_rows(v_ref, at, rows):
     for i in range(0, rows.shape[0], CONV_ROWS):
         p = (at + i) // CONV_ROWS
-        v_ref[p // NXY, p % NXY, 0:CONV_ROWS] = rows[i : i + CONV_ROWS]
-
-
-def kernel_gradients(q_ref, qo_ref, sh_ref, lows, highs, up_ref, hexp_ref, v_ref):
-    down = dot(hexp_ref[...], up_ref[...], NT)
-    for p in range(2 * NXY):
-        v_ref[p // NXY, p % NXY, CONV_ROWS:ROWS] = down[p * 16 : p * 16 + 16]
-    low = jnp.concatenate(lows, 1).astype(BF16)
-    high = jnp.concatenate(highs, 1).astype(BF16)
+        v_ref[p // NXY, p % NXY] = rows[i : i + CONV_ROWS]
+
+
+def conv_gradient(acts, qe_ref, cg_ref, conv_ref):
     plus = []
     for dy in range(3):
-        grads = dot(sh_ref[...], q_ref[dy], NN)
-        grads = jnp.concatenate(
-            [
-                grads[0:64] + dot(low, qo_ref[dy, 0], NN),
-                grads[64:128],
-                grads[128:192] + dot(high, qo_ref[dy, 1], NN),
-            ],
-            0,
-        )
-        put_rows(v_ref, dy * 192, grads[:, 0:128])
+        parts = [
+            cg_ref[dy, dx * 64 : dx * 64 + 64] + dot(acts, qe_ref[dy, dx], NN) for dx in range(3)
+        ]
+        grads = jnp.concatenate(parts, 0)
+        put_rows(conv_ref, dy * 192, grads[:, 0:128])
         plus.append(grads[:, 128:256])
     first = lax.broadcasted_iota(jnp.int32, (192, 128), 1) < 64
-    put_rows(v_ref, 576, jnp.where(first, plus[0], plus[1]))
-    put_rows(v_ref, 768, plus[2])
-    put_rows(v_ref, 960, jnp.zeros((64, 128), F32))
-
-
-def position():
-    s, r = lax.axis_index("space"), lax.axis_index("rep")
-    return s // 8, s // 2 % 4, s % 2 * 2 + r // 2, r % 2
-
-
-def device(z, y, x, core):
-    return {"space": z * 8 + y * 2 + x // 2, "rep": x % 2 * 2 + core}
+    put_rows(conv_ref, 576, jnp.where(first, plus[0], plus[1]))
+    put_rows(conv_ref, 768, plus[2])
+    put_rows(conv_ref, 960, jnp.zeros((64, 128), F32))
+
+
+def remote(src, dst, send, recv, peer):
+    return pltpu.make_async_remote_copy(
+        src, dst, send, recv, device_id=peer, device_id_type=MESH
+    )
 
 
 def section_kernel(
     nb_ref, cnt_ref, f_hbm, g_hbm, cw_hbm, dw_hbm, hid_ref, o_ref,
-    f_ref, g_ref, cw_ref, dw_ref, prev_ref, next_ref, t_ref, lo_ref, hi_ref, q_ref, qo_ref, w_ref,
-    up_ref, grad_ref, pre_ref, hexp_ref, sh_ref,
-    v_ref, mate, outgoing, parts, along, ls, hs, hr, ss, rs, zs, zr, gs, gr, cs, cr,
+    f_ref, g_ref, cw_ref, dw_ref, prev_ref, next_ref, t_ref, lo_ref, hi_ref, q_ref, qe_ref, w_ref,
+    up_ref, grad_ref, pre_ref, hexp_ref, sh_ref, pe_ref, ge_ref, ue_ref, dg_ref, cg_ref,
+    conv_ref, down_ref, mate_conv, mate_down, outgoing, parts, along,
+    ls, hs, hr, cs, cr, ss, rs, zs, zr, gs, gr, es, er,
 ):
-    z, y, x, core = position()
+    strip, tile = lax.axis_index("space"), lax.axis_index("rep")
+    z, rest = lax.div(strip, 8), lax.rem(strip, 8)
+    y, x_hi = lax.div(rest, 2), lax.rem(rest, 2)
+    x_lo, core = lax.div(tile, 2), lax.rem(tile, 2)
+    x = x_hi * 2 + x_lo
     me = y * NX + x
-    sibling = device(z, y, x, 1 - core)
+    sibling = {"space": strip, "rep": x_lo * 2 + 1 - core}
+
+    ys = [y] + [lax.rem(y + d, NY) for d in range(1, NY)]
+    xs = [x] + [lax.rem(x + d, NX) for d in range(1, NX)]
+    x_his = [lax.div(v, 2) for v in xs]
+    tiles = [lax.rem(v, 2) * 2 + core for v in xs]
+    rows = [z * 8 + v * 2 for v in ys]
+    slots = [v * NX for v in ys]
     plane = [(dy, dx) for dy in range(NY) for dx in range(NX) if dy or dx]
     plane.sort(key=lambda o: -(min(o[0], NY - o[0]) + min(o[1], NX - o[1])))
-
-    def plane_peer(o):
-        py, px = (y + o[0]) % NY, (x + o[1]) % NX
-        return device(z, py, px, core), py * NX + px
-
-    def line_peer(dz):
-        return device((z + dz) % NZ, y, x, core)
-
-    strip, tile = lax.axis_index("space"), lax.axis_index("rep")
+    peers = {
+        (dy, dx): ({"space": rows[dy] + x_his[dx], "rep": tiles[dx]}, slots[dy] + xs[dx])
+        for dy, dx in plane
+    }
+    order = [peers[o] for o in plane]
+    line = [{"space": lax.rem(z + d, NZ) * 8 + rest, "rep": tile} for d in (4, 3, 5, 2, 6, 1, 7)]
     strips = NX // 2 * NY * NZ
-    above = {"space": (strip + 1) % strips, "rep": tile}
-    below = {"space": (strip + strips - 1) % strips, "rep": tile}
+    above = {"space": lax.rem(strip + 1, strips), "rep": tile}
+    below = {"space": lax.rem(strip + strips - 1, strips), "rep": tile}
 
     loads = [
         pltpu.make_async_copy(src, dst, ls.at[i])
@@ -231,8 +268,7 @@
     for c in loads:
         c.start()
     barrier = pltpu.get_barrier_semaphore()
-    greet = [above, below] + [plane_peer(o)[0] for o in plane] + [line_peer(d) for d in range(1, NZ)]
-    greet.append(sibling)
+    greet = [above, below] + [peer for peer, _ in order] + line + [sibling]
     for d in greet:
         pl.semaphore_signal(barrier, inc=1, device_id=d, device_id_type=MESH)
     count = cnt_ref[0]
@@ -257,62 +293,55 @@
     loads[2].wait()
     loads[3].wait()
     for b in range(4):
-        fill_inner(nb_ref, count, b, t_ref, q_ref)
+        fill_inner(nb_ref, count, b, t_ref, q_ref, qe_ref)
         cell_gradients(g_ref, dw_ref, count, b, up_ref, grad_ref)
         inner_forward(b, w_ref, q_ref, pre_ref)
+        inner_block(b, pre_ref, grad_ref, hid_ref, hexp_ref, sh_ref)
+    stash_edges(pre_ref, grad_ref, up_ref, pe_ref, ge_ref, ue_ref)
+    dg_ref[...] = dot(hexp_ref[...], up_ref[...], NT)
+    for dy in range(3):
+        cg_ref[dy] = dot(sh_ref[...], q_ref[dy], NN)
 
     for c in halo:
         c.wait()
     fill_halo(prev_ref, next_ref, lo_ref, hi_ref)
     for b in range(4):
-        fill_outer(nb_ref, b, lo_ref, hi_ref, qo_ref)
-    low, high = outer_forward(w_ref, qo_ref)
-    ends = [
-        finish_block(b, low, high, pre_ref, grad_ref, hid_ref, hexp_ref, sh_ref)
-        for b in range(4)
-    ]
-    kernel_gradients(
-        q_ref, qo_ref, sh_ref, [e[0] for e in ends], [e[1] for e in ends], up_ref, hexp_ref, v_ref
-    )
-
-    order = [plane_peer(o) for o in plane]
-    halves = []
-    for i, at in enumerate([at for _, at in order] + [me]):
-        halves.append(
-            pltpu.make_async_remote_copy(
-                v_ref.at[1 - core, at], mate.at[at], cs.at[i], cr.at[i],
-                device_id=sibling, device_id_type=MESH,
-            )
+        fill_outer(nb_ref, b, lo_ref, hi_ref, qe_ref)
+    sums = outer_forward(w_ref, qe_ref)
+
+    acts = edge_planes(sums, pe_ref, ge_ref, ue_ref, hid_ref, dg_ref, down_ref)
+    swap_down = remote(down_ref.at[1 - core], mate_down, cs.at[0], cr.at[0], sibling)
+    swap_down.start()
+    conv_gradient(acts, qe_ref, cg_ref, conv_ref)
+    swap_conv = remote(conv_ref.at[1 - core], mate_conv, cs.at[1], cr.at[1], sibling)
+    swap_conv.start()
+
+    def summed(at):
+        return (
+            conv_ref[core, at] + mate_conv[at],
+            down_ref[core, at] + mate_down[at],
         )
-        halves[-1].start()
+
+    swap_down.wait_recv()
+    swap_conv.wait_recv()
     copies = []
     for i, (peer, at) in enumerate(order):
-        halves[i].wait_recv()
-        outgoing[i] = (v_ref[core, at] + mate[at]).astype(BF16)
-        copies.append(
-            pltpu.make_async_remote_copy(
-                outgoing.at[i], parts.at[i], ss.at[i], rs.at[i],
-                device_id=peer, device_id_type=MESH,
-            )
-        )
+        conv, down = summed(at)
+        outgoing[i, 0:CONV_ROWS] = conv.astype(BF16)
+        outgoing[i, CONV_ROWS:ROWS] = down.astype(BF16)
+        copies.append(remote(outgoing.at[i], parts.at[i], ss.at[i], rs.at[i], peer))
         copies[-1].start()
-    halves[-1].wait_recv()
-    total = v_ref[core, me] + mate[me]
-    for i, c in enumerate(copies):
-        c.wait_recv()
+    total = jnp.concatenate(summed(me), 0)
+    for i in reversed(range(NXY - 1)):
+        copies[i].wait_recv()
         total = total + parts[i].astype(F32)
 
     along[z] = total.astype(BF16)
     lines = []
-    for i, dz in enumerate((4, 3, 5, 2, 6, 1, 7)):
-        lines.append(
-            pltpu.make_async_remote_copy(
-                along.at[z], along.at[z], zs.at[i], zr.at[i],
-                device_id=line_peer(dz), device_id_type=MESH,
-            )
-        )
+    for i, peer in enumerate(line):
+        lines.append(remote(along.at[z], along.at[z], zs.at[i], zr.at[i], peer))
         lines[-1].start()
-    for c in halves + copies:
+    for c in [swap_down, swap_conv] + copies:
         c.wait_send()
     for c in lines:
         c.wait_recv()
@@ -321,32 +350,33 @@
         total = total + along[i].astype(F32)
 
     half = core * NXY
+    own = o_ref.at[half + me]
     o_ref[half + me] = total
     last = []
     for i, (peer, _) in enumerate(order):
-        last.append(
-            pltpu.make_async_remote_copy(
-                o_ref.at[half + me], o_ref.at[half + me], gs.at[i], gr.at[i],
-                device_id=peer, device_id_type=MESH,
-            )
-        )
+        last.append(remote(own, own, gs.at[i], gr.at[i], peer))
         last[-1].start()
+    shared = [remote(own, own, es.at[NXY - 1], er.at[NXY - 1], sibling)]
+    shared[0].start()
     for c in lines:
         c.wait_send()
+    for i in reversed(range(NXY - 1)):
+        last[i].wait_recv()
+        _, at = peers[-plane[i][0] % NY, -plane[i][1] % NX]
+        piece = o_ref.at[half + at]
+        shared.append(remote(piece, piece, es.at[i], er.at[i], sibling))
+        shared[-1].start()
     for c in last:
+        c.wait_send()
+    for c in shared:
         c.wait()
-    rest = pltpu.make_async_remote_copy(
-        o_ref.at[pl.ds(half, NXY)], o_ref.at[pl.ds(half, NXY)], cs.at[NXY], cr.at[NXY],
-        device_id=sibling, device_id_type=MESH,
-    )
-    rest.start()
-    rest.wait()
 
 
 def section(features, neighbours, counts, cotangent, conv_weight, down_weight):
     dma = pltpu.SemaphoreType.DMA
     vm = pltpu.VMEM
     near, line = NXY - 1, NZ - 1
+
     return pl.pallas_call(
         section_kernel,
         out_shape=(
@@ -359,13 +389,16 @@
             vm((4, 64, 512), BF16), vm((4, 64, 128), BF16), vm((27, 64, 64), BF16), vm((8, 64, 128), BF16),
             vm((4, 64, 128), BF16), vm((4, 64, 128), BF16),
             vm((5, 8, 8, 8, 128), F32), vm((9, 8, 8, 128), F32), vm((9, 8, 8, 128), F32),
-            vm((3, 2048, 256), BF16), vm((3, 2, 256, 256), BF16), vm((3, 192, 192), BF16),
+            vm((3, 2048, 256), BF16), vm((3, 3, 512, 256), BF16), vm((3, 192, 192), BF16),
             vm((128, 2048), BF16), vm((4, 64, 512), F32), vm((4, 64, 512), F32),
             vm((512, 2048), BF16), vm((192, 2048), BF16),
-            vm((2, NXY, ROWS, 128), F32), vm((NXY, ROWS, 128), F32),
+            vm((2, 64, 256), F32), vm((2, 64, 256), F32), vm((2, 128, 256), BF16),
+            vm((512, 128), F32), vm((3, 192, 256), F32),
+            vm((2, NXY, CONV_ROWS, 128), F32), vm((2, NXY, DOWN_ROWS, 128), F32),
+            vm((NXY, CONV_ROWS, 128), F32), vm((NXY, DOWN_ROWS, 128), F32),
             vm((near, ROWS, 128), BF16), vm((near, ROWS, 128), BF16), vm((NZ, ROWS, 128), BF16),
-            dma((4,)), dma((2,)), dma((2,)), dma((near,)), dma((near,)), dma((line,)), dma((line,)),
-            dma((near,)), dma((near,)), dma((NXY + 1,)), dma((NXY + 1,)),
+            dma((4,)), dma((2,)), dma((2,)), dma((2,)), dma((2,)), dma((near,)), dma((near,)),
+            dma((line,)), dma((line,)), dma((near,)), dma((near,)), dma((NXY,)), dma((NXY,)),
         ],
         compiler_params=pltpu.CompilerParams(
             collective_id=0, has_side_effects=True, vmem_limit_bytes=56 << 20

time: 42.5 us -> 41.4 us (0.974)
  Pallas kernels: 41.1 us -> 40 us
    pallas_call x1, Pallas kernels: 40 us -> 38.8 us  [section(): pl.pallas_call(section_kernel, out_shape=(pltpu.VMEM((4, 64, 512), BF16),...]
where the time goes in v4:
time: 41.4 us; the launch traced here: 41.2 us
  Pallas kernels  40 us (97%)
  between operations  1.29 us (3%)
    pallas_call x1, Pallas kernels, section(): pl.pallas_call(section_kernel, out_shape=(pltpu.VMEM((4, 64, 512), BF16),...  38.8 us
    pallas_call x1, Pallas kernels, unpack(): pl.pallas_call(unpack_kernel, out_shape=(jax.ShapeDtypeStruct((27, 64, 64...  1.13 us

profile of v4, /device:TPU:1, one launch (start us, length us, event | category | flops | bytes accessed | tf_op | source)
XLA Modules:
  0.0 41.2 jit_solution(4951416434936360489)
XLA Ops:
  1.3 38.8 %section.1 = (bf16[4,64,512]{2,1,0:T(8,128)(2,1)S(1)}, f32[32,48,128]{2,1,0:T(8,128)S(1)}) custom-call(s32[4,27]{1,0:T(4,128)} %nb_ref.1, s32[1]{0:T(128)S(6)} %copy.9.cnt_ref, bf16[4,64,512]{2,1,0:T(8,128)(2,1)} %f_hbm.1, bf16[4,64,128]{2,1,0:T(8,128)(2,1)} %g_hbm.1, bf16[27,64,64]{2,1,0:T(8,128)(2,1)} %cw_hbm.1, bf16[8,64,128]{2,1,0:T(8,128)(2,1)} %bitcast.4), custom_call_target="tpu_custom_call" | custom-call | tf_op jit(solution)/shard_map/section/pallas_call | solution.py:380
  40.1 1.1 %unpack.1 = (f32[27,64,64]{2,1,0:T(8,128)}, f32[32,16,128]{2,1,0:T(8,128)}, bf16[4,64,512]{2,1,0:T(8,128)(2,1)}) custom-call(f32[32,48,128]{2,1,0:T(8,128)S(1)} %get-tuple-element.8.v_ref, bf16[4,64,512]{2,1,0:T(8,128)(2,1)S(1)} %get-tuple-element.9.hid_ref), custom_call_target="tpu_custom_call" | custom-call | tf_op jit(solution)/shard_map/unpack/pallas_call | solution.py:437

commit v5 on v4

--- a/solution.py
+++ b/solution.py
@@ -47,10 +47,26 @@
     hi_ref[8] = jnp.zeros((8, 8, 128), F32)
 
 
-def fill_halo(prev_ref, next_ref, lo_ref, hi_ref):
-    for j in range(4):
-        lo_ref[4 + j] = voxels_in_rows(prev_ref[j])[64:].reshape(8, 8, 128)
-        hi_ref[4 + j] = voxels_in_rows(next_ref[j])[:64].reshape(8, 8, 128)
+def first_half(shape):
+    return lax.broadcasted_iota(jnp.int32, shape, 1) < 64
+
+
+def pack_halo(lo_ref, hi_ref, out_ref):
+    first = first_half((64, 128))
+    for way, table in enumerate((lo_ref, hi_ref)):
+        for j in range(0, 4, 2):
+            pair = [table[j + i].reshape(64, 128) for i in range(2)]
+            out_ref[way, j // 2] = jnp.where(first, *pair).astype(BF16)
+
+
+def fill_halo(in_ref, lo_ref, hi_ref):
+    first = first_half((64, 128))
+    for way, table in enumerate((lo_ref, hi_ref)):
+        for j in range(0, 4, 2):
+            pair = in_ref[way, j // 2].astype(F32)
+            turned = pltpu.roll(pair, 64, 1)
+            table[4 + j] = jnp.where(first, pair, turned).reshape(8, 8, 128)
+            table[5 + j] = jnp.where(first, turned, pair).reshape(8, 8, 128)
 
 
 def store_plane(put, middle, below, above):
@@ -107,25 +123,49 @@
         store_plane(put, *cols)
 
 
-def place_of(shape):
-    v = lax.broadcasted_iota(jnp.int32, shape, 1)
-    return (v // 64 % 2) * 4 + (v // 8 % 2) * 2 + v % 2
-
-
-def cell_gradients(g_ref, dw_ref, count, b, up_ref, grad_ref):
+def regroup(m, outer, inner):
+    first = first_half((64, 128))
+    out = []
+    for i in range(0, inner, 2):
+        even, odd = [], []
+        for o in range(0, outer, 2):
+            x0 = m[o * 64 : o * 64 + 64, i * 64 : i * 64 + 128]
+            x1 = m[o * 64 + 64 : o * 64 + 128, i * 64 : i * 64 + 128]
+            even.append(jnp.where(first, x0, pltpu.roll(x1, 64, 1)))
+            odd.append(jnp.where(first, pltpu.roll(x0, 64, 1), x1))
+        out += [jnp.concatenate(even, 1), jnp.concatenate(odd, 1)]
+    return jnp.concatenate(out, 0)
+
+
+def fill_permutation(s_ref):
     v = lax.broadcasted_iota(jnp.int32, (64, 512), 1)
     u = lax.broadcasted_iota(jnp.int32, (64, 512), 0)
+    place = (v // 64 % 2) * 4 + (v // 8 % 2) * 2 + v % 2
     cell = (v // 128) * 16 + (v // 16 % 4) * 4 + v % 8 // 2
-    spread = (cell == u).astype(F32).astype(BF16)
-    grads = jnp.where(b < count, g_ref[b].astype(F32), 0.0)
-    up = dot(grads.T.astype(BF16), spread, NN).astype(BF16)
-    up_ref[:, b * 512 : b * 512 + 512] = up
-    every = dot(dw_ref[...].reshape(512, 128), up, NN)
-    place = place_of((64, 512))
-    grad = every[0:64]
-    for t in range(1, 8):
-        grad = jnp.where(place == t, every[t * 64 : t * 64 + 64], grad)
-    grad_ref[b] = grad
+    at = place * 64 + cell - u
+    for t in range(8):
+        s_ref[t * 64 : t * 64 + 64] = (at == t * 64).astype(F32).astype(BF16)
+
+
+def cell_gradients(g_ref, dw_ref, count, s_ref, ga_ref, ue_ref, grad_ref):
+    slot = lax.broadcasted_iota(jnp.int32, (256, 128), 0) // 64
+    grads = jnp.where(slot < count, g_ref[...].reshape(256, 128).astype(F32), 0.0)
+    ga_ref[...] = grads.astype(BF16)
+    every = dot(dw_ref[...].reshape(512, 128), ga_ref[...], NT)
+    every = regroup(every, 8, 4).astype(BF16)
+    grad_ref[...] = dot(every, s_ref[...], NN).reshape(4, 64, 512)
+    r = lax.broadcasted_iota(jnp.int32, (256, 256), 0)
+    v = lax.broadcasted_iota(jnp.int32, (256, 256), 1)
+    cell = v // 64 * 64 + v // 16 % 4 * 4 + v % 8 // 2
+    turned = grads.T.astype(BF16)
+    for side in range(2):
+        spread = (r == cell + 48 * side).astype(F32).astype(BF16)
+        ue_ref[side] = dot(turned, spread, NN).astype(BF16)
+
+
+def inner_down(hid_ref, s_ref, ga_ref):
+    cells = dot(hid_ref[...].reshape(256, 512), s_ref[...], NT)
+    return dot(regroup(cells, 4, 8).astype(BF16), ga_ref[...], NN)
 
 
 def inner_forward(b, w_ref, q_ref, pre_ref):
@@ -146,17 +186,14 @@
     return low, high
 
 
-def inner_block(b, pre_ref, grad_ref, hid_ref, hexp_ref, sh_ref):
+def inner_block(b, pre_ref, grad_ref, hid_ref, sh_ref):
     lane = lax.broadcasted_iota(jnp.int32, (64, 512), 1)
     inside = (lane >= 64) & (lane < 448)
     gap = jnp.zeros((64, 64), F32)
     pre = jnp.where(inside, pre_ref[b], 0.0)
     hidden = jnp.maximum(pre, 0.0)
     hid_ref[b] = hidden.astype(BF16)
-    place = place_of((64, 512))
     cols = slice(b * 512, b * 512 + 512)
-    for t in range(8):
-        hexp_ref[t * 64 : t * 64 + 64, cols] = jnp.where(place == t, hidden, 0.0).astype(BF16)
     act = jnp.where(pre > 0, grad_ref[b], 0.0)
     sh_ref[0:64, cols] = jnp.concatenate([act[:, 64:512], gap], 1).astype(BF16)
     sh_ref[64:128, cols] = act.astype(BF16)
@@ -167,13 +204,11 @@
     return slice(448, 512) if side else slice(0, 64)
 
 
-def stash_edges(pre_ref, grad_ref, up_ref, pe_ref, ge_ref, ue_ref):
+def stash_edges(pre_ref, grad_ref, pe_ref, ge_ref):
     for side in range(2):
         at = edge_lanes(side)
         pe_ref[side] = jnp.concatenate([pre_ref[b, :, at] for b in range(4)], 1)
         ge_ref[side] = jnp.concatenate([grad_ref[b, :, at] for b in range(4)], 1)
-        ups = [up_ref[:, b * 512 + at.start : b * 512 + at.stop].astype(F32) for b in range(4)]
-        ue_ref[side] = jnp.concatenate(ups, 1).astype(BF16)
 
 
 def edge_planes(sums, pe_ref, ge_ref, ue_ref, hid_ref, dg_ref, down_ref):
@@ -228,8 +263,8 @@
 
 def section_kernel(
     nb_ref, cnt_ref, f_hbm, g_hbm, cw_hbm, dw_hbm, hid_ref, o_ref,
-    f_ref, g_ref, cw_ref, dw_ref, prev_ref, next_ref, t_ref, lo_ref, hi_ref, q_ref, qe_ref, w_ref,
-    up_ref, grad_ref, pre_ref, hexp_ref, sh_ref, pe_ref, ge_ref, ue_ref, dg_ref, cg_ref,
+    f_ref, g_ref, cw_ref, dw_ref, ho_ref, hi_in_ref, t_ref, lo_ref, hi_ref, q_ref, qe_ref, w_ref,
+    s_ref, ga_ref, grad_ref, pre_ref, sh_ref, pe_ref, ge_ref, ue_ref, dg_ref, cg_ref,
     conv_ref, down_ref, mate_conv, mate_down, outgoing, parts, along,
     ls, hs, hr, cs, cr, ss, rs, zs, zr, gs, gr, es, er,
 ):
@@ -275,14 +310,15 @@
 
     loads[0].wait()
     fill_tables(f_ref, t_ref, lo_ref, hi_ref)
+    pack_halo(lo_ref, hi_ref, ho_ref)
     pl.semaphore_wait(barrier, len(greet))
     halo = [
         pltpu.make_async_remote_copy(
-            f_ref.at[:, :, pl.ds(384, 128)], prev_ref, hs.at[0], hr.at[0],
+            ho_ref.at[0], hi_in_ref.at[0], hs.at[0], hr.at[0],
             device_id=above, device_id_type=MESH,
         ),
         pltpu.make_async_remote_copy(
-            f_ref.at[:, :, pl.ds(0, 128)], next_ref, hs.at[1], hr.at[1],
+            ho_ref.at[1], hi_in_ref.at[1], hs.at[1], hr.at[1],
             device_id=below, device_id_type=MESH,
         ),
     ]
@@ -290,21 +326,22 @@
         c.start()
     loads[1].wait()
     fill_weights(cw_ref, w_ref)
+    fill_permutation(s_ref)
     loads[2].wait()
     loads[3].wait()
+    cell_gradients(g_ref, dw_ref, count, s_ref, ga_ref, ue_ref, grad_ref)
     for b in range(4):
         fill_inner(nb_ref, count, b, t_ref, q_ref, qe_ref)
-        cell_gradients(g_ref, dw_ref, count, b, up_ref, grad_ref)
         inner_forward(b, w_ref, q_ref, pre_ref)
-        inner_block(b, pre_ref, grad_ref, hid_ref, hexp_ref, sh_ref)
-    stash_edges(pre_ref, grad_ref, up_ref, pe_ref, ge_ref, ue_ref)
-    dg_ref[...] = dot(hexp_ref[...], up_ref[...], NT)
+        inner_block(b, pre_ref, grad_ref, hid_ref, sh_ref)
+    stash_edges(pre_ref, grad_ref, pe_ref, ge_ref)
+    dg_ref[...] = inner_down(hid_ref, s_ref, ga_ref)
     for dy in range(3):
         cg_ref[dy] = dot(sh_ref[...], q_ref[dy], NN)
 
     for c in halo:
         c.wait()
-    fill_halo(prev_ref, next_ref, lo_ref, hi_ref)
+    fill_halo(hi_in_ref, lo_ref, hi_ref)
     for b in range(4):
         fill_outer(nb_ref, b, lo_ref, hi_ref, qe_ref)
     sums = outer_forward(w_ref, qe_ref)
@@ -387,11 +424,11 @@
         out_specs=(VM, VM),
         scratch_shapes=[
             vm((4, 64, 512), BF16), vm((4, 64, 128), BF16), vm((27, 64, 64), BF16), vm((8, 64, 128), BF16),
-            vm((4, 64, 128), BF16), vm((4, 64, 128), BF16),
+            vm((2, 2, 64, 128), BF16), vm((2, 2, 64, 128), BF16),
             vm((5, 8, 8, 8, 128), F32), vm((9, 8, 8, 128), F32), vm((9, 8, 8, 128), F32),
             vm((3, 2048, 256), BF16), vm((3, 3, 512, 256), BF16), vm((3, 192, 192), BF16),
-            vm((128, 2048), BF16), vm((4, 64, 512), F32), vm((4, 64, 512), F32),
-            vm((512, 2048), BF16), vm((192, 2048), BF16),
+            vm((512, 512), BF16), vm((256, 128), BF16), vm((4, 64, 512), F32), vm((4, 64, 512), F32),
+            vm((192, 2048), BF16),
             vm((2, 64, 256), F32), vm((2, 64, 256), F32), vm((2, 128, 256), BF16),
             vm((512, 128), F32), vm((3, 192, 256), F32),
             vm((2, NXY, CONV_ROWS, 128), F32), vm((2, NXY, DOWN_ROWS, 128), F32),

time: 41.4 us -> 40.9 us (0.988)
  Pallas kernels: 40 us -> 39.4 us
    pallas_call x1, Pallas kernels: 38.8 us -> 38.3 us  [section(): pl.pallas_call(section_kernel, out_shape=(pltpu.VMEM((4, 64, 512), BF16),...]
where the time goes in v5:
time: 40.9 us; the launch traced here: 40.7 us
  Pallas kernels  39.4 us (96%)
  between operations  1.29 us (3%)
    pallas_call x1, Pallas kernels, section(): pl.pallas_call(section_kernel, out_shape=(pltpu.VMEM((4, 64, 512), BF16),...  38.3 us
    pallas_call x1, Pallas kernels, unpack(): pl.pallas_call(unpack_kernel, out_shape=(jax.ShapeDtypeStruct((27, 64, 64...  1.13 us

profile of v5, /device:TPU:1, one launch (start us, length us, event | category | flops | bytes accessed | tf_op | source)
XLA Modules:
  0.0 40.7 jit_solution(10497711851436139509)
XLA Ops:
  1.3 38.3 %section.1 = (bf16[4,64,512]{2,1,0:T(8,128)(2,1)S(1)}, f32[32,48,128]{2,1,0:T(8,128)S(1)}) custom-call(s32[4,27]{1,0:T(4,128)} %nb_ref.1, s32[1]{0:T(128)S(6)} %copy.9.cnt_ref, bf16[4,64,512]{2,1,0:T(8,128)(2,1)} %f_hbm.1, bf16[4,64,128]{2,1,0:T(8,128)(2,1)} %g_hbm.1, bf16[27,64,64]{2,1,0:T(8,128)(2,1)} %cw_hbm.1, bf16[8,64,128]{2,1,0:T(8,128)(2,1)} %bitcast.4), custom_call_target="tpu_custom_call" | custom-call | tf_op jit(solution)/shard_map/section/pallas_call | solution.py:417
  39.6 1.1 %unpack.1 = (f32[27,64,64]{2,1,0:T(8,128)}, f32[32,16,128]{2,1,0:T(8,128)}, bf16[4,64,512]{2,1,0:T(8,128)(2,1)}) custom-call(f32[32,48,128]{2,1,0:T(8,128)S(1)} %get-tuple-element.8.v_ref, bf16[4,64,512]{2,1,0:T(8,128)(2,1)S(1)} %get-tuple-element.9.hid_ref), custom_call_target="tpu_custom_call" | custom-call | tf_op jit(solution)/shard_map/unpack/pallas_call | solution.py:474

commit v6 on v5

--- a/solution.py
+++ b/solution.py
@@ -8,7 +8,6 @@
 MESH = pl.DeviceIdType.MESH
 F32, BF16 = jnp.float32, jnp.bfloat16
 VM = pl.BlockSpec(memory_space=pltpu.VMEM)
-SM = pl.BlockSpec(memory_space=pltpu.SMEM)
 ANY = pl.BlockSpec(memory_space=pl.ANY)
 NX, NY, NZ = 4, 4, 8
 NXY = NX * NY
@@ -262,8 +261,8 @@
 
 
 def section_kernel(
-    nb_ref, cnt_ref, f_hbm, g_hbm, cw_hbm, dw_hbm, hid_ref, o_ref,
-    f_ref, g_ref, cw_ref, dw_ref, ho_ref, hi_in_ref, t_ref, lo_ref, hi_ref, q_ref, qe_ref, w_ref,
+    nb_hbm, cnt_hbm, f_hbm, g_hbm, cw_hbm, dw_hbm, hid_ref, o_ref,
+    nb_ref, cnt_ref, f_ref, g_ref, cw_ref, dw_ref, ho_ref, hi_in_ref, t_ref, lo_ref, hi_ref, q_ref, qe_ref, w_ref,
     s_ref, ga_ref, grad_ref, pre_ref, sh_ref, pe_ref, ge_ref, ue_ref, dg_ref, cg_ref,
     conv_ref, down_ref, mate_conv, mate_down, outgoing, parts, along,
     ls, hs, hr, cs, cr, ss, rs, zs, zr, gs, gr, es, er,
@@ -297,16 +296,17 @@
     loads = [
         pltpu.make_async_copy(src, dst, ls.at[i])
         for i, (src, dst) in enumerate(
-            ((f_hbm, f_ref), (cw_hbm, cw_ref), (g_hbm, g_ref), (dw_hbm, dw_ref))
+            ((f_hbm, f_ref), (cw_hbm, cw_ref), (g_hbm, g_ref), (dw_hbm, dw_ref), (nb_hbm, nb_ref), (cnt_hbm, cnt_ref))
         )
     ]
-    for c in loads:
-        c.start()
+    loads[0].start()
     barrier = pltpu.get_barrier_semaphore()
     greet = [above, below] + [peer for peer, _ in order] + line + [sibling]
-    for d in greet:
+    for i, d in enumerate(greet):
         pl.semaphore_signal(barrier, inc=1, device_id=d, device_id_type=MESH)
-    count = cnt_ref[0]
+        if i == 1:
+            for c in loads[1:]:
+                c.start()
 
     loads[0].wait()
     fill_tables(f_ref, t_ref, lo_ref, hi_ref)
@@ -327,8 +327,9 @@
     loads[1].wait()
     fill_weights(cw_ref, w_ref)
     fill_permutation(s_ref)
-    loads[2].wait()
-    loads[3].wait()
+    for c in loads[2:]:
+        c.wait()
+    count = cnt_ref[0]
     cell_gradients(g_ref, dw_ref, count, s_ref, ga_ref, ue_ref, grad_ref)
     for b in range(4):
         fill_inner(nb_ref, count, b, t_ref, q_ref, qe_ref)
@@ -420,9 +421,10 @@
             pltpu.VMEM((4, 64, 512), BF16),
             pltpu.VMEM((32, ROWS, 128), F32),
         ),
-        in_specs=[SM, SM, ANY, ANY, ANY, ANY],
+        in_specs=[ANY] * 6,
         out_specs=(VM, VM),
         scratch_shapes=[
+            pltpu.SMEM((4, 27), jnp.int32), pltpu.SMEM((1,), jnp.int32),
             vm((4, 64, 512), BF16), vm((4, 64, 128), BF16), vm((27, 64, 64), BF16), vm((8, 64, 128), BF16),
             vm((2, 2, 64, 128), BF16), vm((2, 2, 64, 128), BF16),
             vm((5, 8, 8, 8, 128), F32), vm((9, 8, 8, 128), F32), vm((9, 8, 8, 128), F32),
@@ -434,7 +436,7 @@
             vm((2, NXY, CONV_ROWS, 128), F32), vm((2, NXY, DOWN_ROWS, 128), F32),
             vm((NXY, CONV_ROWS, 128), F32), vm((NXY, DOWN_ROWS, 128), F32),
             vm((near, ROWS, 128), BF16), vm((near, ROWS, 128), BF16), vm((NZ, ROWS, 128), BF16),
-            dma((4,)), dma((2,)), dma((2,)), dma((2,)), dma((2,)), dma((near,)), dma((near,)),
+            dma((6,)), dma((2,)), dma((2,)), dma((2,)), dma((2,)), dma((near,)), dma((near,)),
             dma((line,)), dma((line,)), dma((near,)), dma((near,)), dma((NXY,)), dma((NXY,)),
         ],
         compiler_params=pltpu.CompilerParams(

time: 40.9 us -> 40.1 us (0.980)
  Pallas kernels: 39.4 us -> 38.7 us
    pallas_call x1, Pallas kernels: 38.3 us -> 37.6 us  [section(): pl.pallas_call(section_kernel, out_shape=(pltpu.VMEM((4, 64, 512), BF16),...]
where the time goes in v6:
time: 40.1 us; the launch traced here: 40 us
  Pallas kernels  38.7 us (97%)
  between operations  1.29 us (3%)
    pallas_call x1, Pallas kernels, section(): pl.pallas_call(section_kernel, out_shape=(pltpu.VMEM((4, 64, 512), BF16),...  37.6 us
    pallas_call x1, Pallas kernels, unpack(): pl.pallas_call(unpack_kernel, out_shape=(jax.ShapeDtypeStruct((27, 64, 64...  1.13 us

profile of v6, /device:TPU:1, one launch (start us, length us, event | category | flops | bytes accessed | tf_op | source)
XLA Modules:
  0.0 40.0 jit_solution(2455813832571370836)
XLA Ops:
  1.3 37.6 %section.1 = (bf16[4,64,512]{2,1,0:T(8,128)(2,1)S(1)}, f32[32,48,128]{2,1,0:T(8,128)S(1)}) custom-call(s32[4,27]{1,0:T(4,128)} %nb_hbm.1, s32[1]{0:T(128)S(6)} %copy.9.cnt_hbm, bf16[4,64,512]{2,1,0:T(8,128)(2,1)} %f_hbm.1, bf16[4,64,128]{2,1,0:T(8,128)(2,1)} %g_hbm.1, bf16[27,64,64]{2,1,0:T(8,128)(2,1)} %cw_hbm.1, bf16[8,64,128]{2,1,0:T(8,128)(2,1)} %bitcast.4), custom_call_target="tpu_custom_call" | custom-call | tf_op jit(solution)/shard_map/section/pallas_call | solution.py:418
  38.9 1.1 %unpack.1 = (f32[27,64,64]{2,1,0:T(8,128)}, f32[32,16,128]{2,1,0:T(8,128)}, bf16[4,64,512]{2,1,0:T(8,128)(2,1)}) custom-call(f32[32,48,128]{2,1,0:T(8,128)S(1)} %get-tuple-element.8.v_ref, bf16[4,64,512]{2,1,0:T(8,128)(2,1)S(1)} %get-tuple-element.9.hid_ref), custom_call_target="tpu_custom_call" | custom-call | tf_op jit(solution)/shard_map/unpack/pallas_call | solution.py:476

commit v7 on v6

--- a/solution.py
+++ b/solution.py
@@ -362,27 +362,26 @@
 
     swap_down.wait_recv()
     swap_conv.wait_recv()
-    copies = []
     for i, (peer, at) in enumerate(order):
         conv, down = summed(at)
         outgoing[i, 0:CONV_ROWS] = conv.astype(BF16)
         outgoing[i, CONV_ROWS:ROWS] = down.astype(BF16)
-        copies.append(remote(outgoing.at[i], parts.at[i], ss.at[i], rs.at[i], peer))
-        copies[-1].start()
+        remote(outgoing.at[i], parts.at[i], ss.at[0], rs.at[0], peer).start()
     total = jnp.concatenate(summed(me), 0)
-    for i in reversed(range(NXY - 1)):
-        copies[i].wait_recv()
+    scattered = remote(outgoing, parts, ss.at[0], rs.at[0], sibling)
+    scattered.wait_recv()
+    for i in range(NXY - 1):
         total = total + parts[i].astype(F32)
 
     along[z] = total.astype(BF16)
-    lines = []
-    for i, peer in enumerate(line):
-        lines.append(remote(along.at[z], along.at[z], zs.at[i], zr.at[i], peer))
-        lines[-1].start()
-    for c in [swap_down, swap_conv] + copies:
-        c.wait_send()
-    for c in lines:
-        c.wait_recv()
+    for peer in line:
+        remote(along.at[z], along.at[z], zs.at[0], zr.at[0], peer).start()
+    swap_down.wait_send()
+    swap_conv.wait_send()
+    scattered.wait_send()
+    most = along.at[pl.ds(0, NZ - 1)]
+    spread = remote(most, most, zs.at[0], zr.at[0], sibling)
+    spread.wait_recv()
     total = along[0].astype(F32)
     for i in range(1, NZ):
         total = total + along[i].astype(F32)
@@ -392,28 +391,25 @@
     o_ref[half + me] = total
     last = []
     for i, (peer, _) in enumerate(order):
-        last.append(remote(own, own, gs.at[i], gr.at[i], peer))
+        last.append(remote(own, own, gs.at[0], gr.at[i], peer))
         last[-1].start()
-    shared = [remote(own, own, es.at[NXY - 1], er.at[NXY - 1], sibling)]
-    shared[0].start()
-    for c in lines:
-        c.wait_send()
+    remote(own, own, es.at[0], er.at[0], sibling).start()
+    spread.wait_send()
     for i in reversed(range(NXY - 1)):
         last[i].wait_recv()
         _, at = peers[-plane[i][0] % NY, -plane[i][1] % NX]
         piece = o_ref.at[half + at]
-        shared.append(remote(piece, piece, es.at[i], er.at[i], sibling))
-        shared[-1].start()
-    for c in last:
-        c.wait_send()
-    for c in shared:
-        c.wait()
+        remote(piece, piece, es.at[0], er.at[0], sibling).start()
+    sent = o_ref.at[pl.ds(half, NXY - 1)]
+    remote(sent, sent, gs.at[0], gr.at[0], sibling).wait_send()
+    block = o_ref.at[pl.ds(half, NXY)]
+    remote(block, block, es.at[0], er.at[0], sibling).wait()
 
 
 def section(features, neighbours, counts, cotangent, conv_weight, down_weight):
     dma = pltpu.SemaphoreType.DMA
     vm = pltpu.VMEM
-    near, line = NXY - 1, NZ - 1
+    near = NXY - 1
 
     return pl.pallas_call(
         section_kernel,
@@ -436,8 +432,8 @@
             vm((2, NXY, CONV_ROWS, 128), F32), vm((2, NXY, DOWN_ROWS, 128), F32),
             vm((NXY, CONV_ROWS, 128), F32), vm((NXY, DOWN_ROWS, 128), F32),
             vm((near, ROWS, 128), BF16), vm((near, ROWS, 128), BF16), vm((NZ, ROWS, 128), BF16),
-            dma((6,)), dma((2,)), dma((2,)), dma((2,)), dma((2,)), dma((near,)), dma((near,)),
-            dma((line,)), dma((line,)), dma((near,)), dma((near,)), dma((NXY,)), dma((NXY,)),
+            dma((6,)), dma((2,)), dma((2,)), dma((2,)), dma((2,)), dma((1,)), dma((1,)),
+            dma((1,)), dma((1,)), dma((1,)), dma((near,)), dma((1,)), dma((1,)),
         ],
         compiler_params=pltpu.CompilerParams(
             collective_id=0, has_side_effects=True, vmem_limit_bytes=56 << 20

time: 40.1 us -> 39.4 us (0.983)
  Pallas kernels: 38.7 us -> 38 us
    pallas_call x1, Pallas kernels: 37.6 us -> 36.8 us  [section(): pl.pallas_call(section_kernel, out_shape=(pltpu.VMEM((4, 64, 512), BF16),...]
where the time goes in v7:
time: 39.4 us; the launch traced here: 39.3 us
  Pallas kernels  38 us (96%)
  between operations  1.29 us (3%)
    pallas_call x1, Pallas kernels, section(): pl.pallas_call(section_kernel, out_shape=(pltpu.VMEM((4, 64, 512), BF16),...  36.8 us
    pallas_call x1, Pallas kernels, unpack(): pl.pallas_call(unpack_kernel, out_shape=(jax.ShapeDtypeStruct((27, 64, 64...  1.13 us

profile of v7, /device:TPU:1, one launch (start us, length us, event | category | flops | bytes accessed | tf_op | source)
XLA Modules:
  0.0 39.3 jit_solution(17285248368018841525)
XLA Ops:
  1.3 36.8 %section.1 = (bf16[4,64,512]{2,1,0:T(8,128)(2,1)S(1)}, f32[32,48,128]{2,1,0:T(8,128)S(1)}) custom-call(s32[4,27]{1,0:T(4,128)} %nb_hbm.1, s32[1]{0:T(128)S(6)} %copy.9.cnt_hbm, bf16[4,64,512]{2,1,0:T(8,128)(2,1)} %f_hbm.1, bf16[4,64,128]{2,1,0:T(8,128)(2,1)} %g_hbm.1, bf16[27,64,64]{2,1,0:T(8,128)(2,1)} %cw_hbm.1, bf16[8,64,128]{2,1,0:T(8,128)(2,1)} %bitcast.4), custom_call_target="tpu_custom_call" | custom-call | tf_op jit(solution)/shard_map/section/pallas_call | solution.py:414
  38.1 1.1 %unpack.1 = (f32[27,64,64]{2,1,0:T(8,128)}, f32[32,16,128]{2,1,0:T(8,128)}, bf16[4,64,512]{2,1,0:T(8,128)(2,1)}) custom-call(f32[32,48,128]{2,1,0:T(8,128)S(1)} %get-tuple-element.8.v_ref, bf16[4,64,512]{2,1,0:T(8,128)(2,1)S(1)} %get-tuple-element.9.hid_ref), custom_call_target="tpu_custom_call" | custom-call | tf_op jit(solution)/shard_map/unpack/pallas_call | solution.py:472

commit v8 on v7

--- a/solution.py
+++ b/solution.py
@@ -283,6 +283,7 @@
     slots = [v * NX for v in ys]
     plane = [(dy, dx) for dy in range(NY) for dx in range(NX) if dy or dx]
     plane.sort(key=lambda o: -(min(o[0], NY - o[0]) + min(o[1], NX - o[1])))
+    plane = [plane[i] for i in (0, 1, 4, 2, 3, 6, 7, 9, 10, 5, 8, 11, 14, 12, 13)]
     peers = {
         (dy, dx): ({"space": rows[dy] + x_his[dx], "rep": tiles[dx]}, slots[dy] + xs[dx])
         for dy, dx in plane

time: 39.4 us -> 39.2 us (level)
  no operation moved by 1% of the time
where the time goes in v8:
time: 39.2 us; the launch traced here: 39.1 us
  Pallas kernels  37.8 us (96%)
  between operations  1.29 us (3%)
    pallas_call x1, Pallas kernels, section(): pl.pallas_call(section_kernel, out_shape=(pltpu.VMEM((4, 64, 512), BF16),...  36.6 us
    pallas_call x1, Pallas kernels, unpack(): pl.pallas_call(unpack_kernel, out_shape=(jax.ShapeDtypeStruct((27, 64, 64...  1.13 us

profile of v8, /device:TPU:1, one launch (start us, length us, event | category | flops | bytes accessed | tf_op | source)
XLA Modules:
  0.0 39.1 jit_solution(12510715293102359375)
XLA Ops:
  1.3 36.6 %section.1 = (bf16[4,64,512]{2,1,0:T(8,128)(2,1)S(1)}, f32[32,48,128]{2,1,0:T(8,128)S(1)}) custom-call(s32[4,27]{1,0:T(4,128)} %nb_hbm.1, s32[1]{0:T(128)S(6)} %copy.9.cnt_hbm, bf16[4,64,512]{2,1,0:T(8,128)(2,1)} %f_hbm.1, bf16[4,64,128]{2,1,0:T(8,128)(2,1)} %g_hbm.1, bf16[27,64,64]{2,1,0:T(8,128)(2,1)} %cw_hbm.1, bf16[8,64,128]{2,1,0:T(8,128)(2,1)} %bitcast.4), custom_call_target="tpu_custom_call" | custom-call | tf_op jit(solution)/shard_map/section/pallas_call | solution.py:415
  37.9 1.1 %unpack.1 = (f32[27,64,64]{2,1,0:T(8,128)}, f32[32,16,128]{2,1,0:T(8,128)}, bf16[4,64,512]{2,1,0:T(8,128)(2,1)}) custom-call(f32[32,48,128]{2,1,0:T(8,128)S(1)} %get-tuple-element.8.v_ref, bf16[4,64,512]{2,1,0:T(8,128)(2,1)S(1)} %get-tuple-element.9.hid_ref), custom_call_target="tpu_custom_call" | custom-call | tf_op jit(solution)/shard_map/unpack/pallas_call | solution.py:473

commit v9 on v8

--- a/solution.py
+++ b/solution.py
@@ -13,6 +13,7 @@
 NXY = NX * NY
 CONV_ROWS, DOWN_ROWS = 32, 16
 ROWS = CONV_ROWS + DOWN_ROWS
+FAR = 5
 
 
 def dot(a, b, dims):
@@ -210,10 +211,9 @@
         ge_ref[side] = jnp.concatenate([grad_ref[b, :, at] for b in range(4)], 1)
 
 
-def edge_planes(sums, pe_ref, ge_ref, ue_ref, hid_ref, dg_ref, down_ref):
+def edge_planes(sums, pe_ref, ge_ref, ue_ref, dg_ref, down_ref):
     v = lax.broadcasted_iota(jnp.int32, (64, 256), 1)
     place = (v // 8 % 2) * 2 + v % 2
-    first = lax.broadcasted_iota(jnp.int32, (64, 128), 1) < 64
     acts = []
     for side in range(2):
         pre = pe_ref[side] + sums[side]
@@ -223,6 +223,13 @@
         down = dg_ref[side * 256 : side * 256 + 256] + dot(spread.astype(BF16), ue_ref[side], NT)
         for p in range(NXY):
             down_ref[side, p] = down[p * 16 : p * 16 + 16]
+    return jnp.concatenate(acts, 1).astype(BF16)
+
+
+def edge_hidden(sums, pe_ref, hid_ref):
+    first = first_half((64, 128))
+    for side in range(2):
+        hidden = jnp.maximum(pe_ref[side] + sums[side], 0.0)
         tile = slice(384, 512) if side else slice(0, 128)
         for b in range(4):
             mine = hidden[:, b // 2 * 128 : b // 2 * 128 + 128]
@@ -230,7 +237,6 @@
                 mine = pltpu.roll(mine, 64, 1)
             old = hid_ref[b, :, tile].astype(F32)
             hid_ref[b, :, tile] = jnp.where(first != (side == 1), mine, old).astype(BF16)
-    return jnp.concatenate(acts, 1).astype(BF16)
 
 
 def put_rows(v_ref, at, rows):
@@ -264,8 +270,8 @@
     nb_hbm, cnt_hbm, f_hbm, g_hbm, cw_hbm, dw_hbm, hid_ref, o_ref,
     nb_ref, cnt_ref, f_ref, g_ref, cw_ref, dw_ref, ho_ref, hi_in_ref, t_ref, lo_ref, hi_ref, q_ref, qe_ref, w_ref,
     s_ref, ga_ref, grad_ref, pre_ref, sh_ref, pe_ref, ge_ref, ue_ref, dg_ref, cg_ref,
-    conv_ref, down_ref, mate_conv, mate_down, outgoing, parts, along,
-    ls, hs, hr, cs, cr, ss, rs, zs, zr, gs, gr, es, er,
+    conv_ref, down_ref, mate_conv, mate_down, outgoing, parts, far_out, far_in, along,
+    ls, hs, hr, cs, cr, ss, rs, zs, zr, gs, gr, es, er, fs, fr,
 ):
     strip, tile = lax.axis_index("space"), lax.axis_index("rep")
     z, rest = lax.div(strip, 8), lax.rem(strip, 8)
@@ -289,6 +295,8 @@
         for dy, dx in plane
     }
     order = [peers[o] for o in plane]
+    far = order[:FAR]
+    crossed = [{"space": rows[dy] + x_his[dx], "rep": tiles[dx] + 1 - 2 * core} for dy, dx in plane[:FAR]]
     line = [{"space": lax.rem(z + d, NZ) * 8 + rest, "rep": tile} for d in (4, 3, 5, 2, 6, 1, 7)]
     strips = NX // 2 * NY * NZ
     above = {"space": lax.rem(strip + 1, strips), "rep": tile}
@@ -302,7 +310,7 @@
     ]
     loads[0].start()
     barrier = pltpu.get_barrier_semaphore()
-    greet = [above, below] + [peer for peer, _ in order] + line + [sibling]
+    greet = [above, below] + [peer for peer, _ in order] + crossed + line + [sibling]
     for i, d in enumerate(greet):
         pl.semaphore_signal(barrier, inc=1, device_id=d, device_id_type=MESH)
         if i == 1:
@@ -348,10 +356,16 @@
         fill_outer(nb_ref, b, lo_ref, hi_ref, qe_ref)
     sums = outer_forward(w_ref, qe_ref)
 
-    acts = edge_planes(sums, pe_ref, ge_ref, ue_ref, hid_ref, dg_ref, down_ref)
+    acts = edge_planes(sums, pe_ref, ge_ref, ue_ref, dg_ref, down_ref)
     swap_down = remote(down_ref.at[1 - core], mate_down, cs.at[0], cr.at[0], sibling)
     swap_down.start()
     conv_gradient(acts, qe_ref, cg_ref, conv_ref)
+    for i, (peer, at) in enumerate(far):
+        for k, (half, target) in enumerate(((core, peer), (1 - core, crossed[i]))):
+            slot = 2 * i + k
+            far_out[slot, 0:CONV_ROWS] = conv_ref[half, at].astype(BF16)
+            far_out[slot, CONV_ROWS:ROWS] = down_ref[half, at].astype(BF16)
+            remote(far_out.at[slot], far_in.at[slot], fs.at[0], fr.at[0], target).start()
     swap_conv = remote(conv_ref.at[1 - core], mate_conv, cs.at[1], cr.at[1], sibling)
     swap_conv.start()
 
@@ -363,7 +377,7 @@
 
     swap_down.wait_recv()
     swap_conv.wait_recv()
-    for i, (peer, at) in enumerate(order):
+    for i, (peer, at) in enumerate(order[FAR:]):
         conv, down = summed(at)
         outgoing[i, 0:CONV_ROWS] = conv.astype(BF16)
         outgoing[i, CONV_ROWS:ROWS] = down.astype(BF16)
@@ -371,15 +385,21 @@
     total = jnp.concatenate(summed(me), 0)
     scattered = remote(outgoing, parts, ss.at[0], rs.at[0], sibling)
     scattered.wait_recv()
-    for i in range(NXY - 1):
+    for i in range(NXY - 1 - FAR):
         total = total + parts[i].astype(F32)
+    straight = remote(far_out, far_in, fs.at[0], fr.at[0], sibling)
+    straight.wait_recv()
+    for i in range(2 * FAR):
+        total = total + far_in[i].astype(F32)
 
     along[z] = total.astype(BF16)
     for peer in line:
         remote(along.at[z], along.at[z], zs.at[0], zr.at[0], peer).start()
+    edge_hidden(sums, pe_ref, hid_ref)
     swap_down.wait_send()
     swap_conv.wait_send()
     scattered.wait_send()
+    straight.wait_send()
     most = along.at[pl.ds(0, NZ - 1)]
     spread = remote(most, most, zs.at[0], zr.at[0], sibling)
     spread.wait_recv()
@@ -432,9 +452,10 @@
             vm((512, 128), F32), vm((3, 192, 256), F32),
             vm((2, NXY, CONV_ROWS, 128), F32), vm((2, NXY, DOWN_ROWS, 128), F32),
             vm((NXY, CONV_ROWS, 128), F32), vm((NXY, DOWN_ROWS, 128), F32),
-            vm((near, ROWS, 128), BF16), vm((near, ROWS, 128), BF16), vm((NZ, ROWS, 128), BF16),
+            vm((near - FAR, ROWS, 128), BF16), vm((near - FAR, ROWS, 128), BF16),
+            vm((2 * FAR, ROWS, 128), BF16), vm((2 * FAR, ROWS, 128), BF16), vm((NZ, ROWS, 128), BF16),
             dma((6,)), dma((2,)), dma((2,)), dma((2,)), dma((2,)), dma((1,)), dma((1,)),
-            dma((1,)), dma((1,)), dma((1,)), dma((near,)), dma((1,)), dma((1,)),
+            dma((1,)), dma((1,)), dma((1,)), dma((near,)), dma((1,)), dma((1,)), dma((1,)), dma((1,)),
         ],
         compiler_params=pltpu.CompilerParams(
             collective_id=0, has_side_effects=True, vmem_limit_bytes=56 << 20

time: 39.2 us -> 39.4 us (level)
  no operation moved by 1% of the time
where the time goes in v9:
time: 39.4 us; the launch traced here: 39.2 us
  Pallas kernels  38 us (96%)
  between operations  1.29 us (3%)
    pallas_call x1, Pallas kernels, section(): pl.pallas_call(section_kernel, out_shape=(pltpu.VMEM((4, 64, 512), BF16),...  36.8 us
    pallas_call x1, Pallas kernels, unpack(): pl.pallas_call(unpack_kernel, out_shape=(jax.ShapeDtypeStruct((27, 64, 64...  1.13 us

profile of v9, /device:TPU:1, one launch (start us, length us, event | category | flops | bytes accessed | tf_op | source)
XLA Modules:
  0.0 39.2 jit_solution(7109046297034057563)
XLA Ops:
  1.3 36.8 %section.1 = (bf16[4,64,512]{2,1,0:T(8,128)(2,1)S(1)}, f32[32,48,128]{2,1,0:T(8,128)S(1)}) custom-call(s32[4,27]{1,0:T(4,128)} %nb_hbm.1, s32[1]{0:T(128)S(6)} %copy.9.cnt_hbm, bf16[4,64,512]{2,1,0:T(8,128)(2,1)} %f_hbm.1, bf16[4,64,128]{2,1,0:T(8,128)(2,1)} %g_hbm.1, bf16[27,64,64]{2,1,0:T(8,128)(2,1)} %cw_hbm.1, bf16[8,64,128]{2,1,0:T(8,128)(2,1)} %bitcast.4), custom_call_target="tpu_custom_call" | custom-call | tf_op jit(solution)/shard_map/section/pallas_call | solution.py:435
  38.1 1.1 %unpack.1 = (f32[27,64,64]{2,1,0:T(8,128)}, f32[32,16,128]{2,1,0:T(8,128)}, bf16[4,64,512]{2,1,0:T(8,128)(2,1)}) custom-call(f32[32,48,128]{2,1,0:T(8,128)S(1)} %get-tuple-element.8.v_ref, bf16[4,64,512]{2,1,0:T(8,128)(2,1)S(1)} %get-tuple-element.9.hid_ref), custom_call_target="tpu_custom_call" | custom-call | tf_op jit(solution)/shard_map/unpack/pallas_call | solution.py:494

commit v10 on v8

--- a/solution.py
+++ b/solution.py
@@ -210,10 +210,9 @@
         ge_ref[side] = jnp.concatenate([grad_ref[b, :, at] for b in range(4)], 1)
 
 
-def edge_planes(sums, pe_ref, ge_ref, ue_ref, hid_ref, dg_ref, down_ref):
+def edge_planes(sums, pe_ref, ge_ref, ue_ref, dg_ref, down_ref):
     v = lax.broadcasted_iota(jnp.int32, (64, 256), 1)
     place = (v // 8 % 2) * 2 + v % 2
-    first = lax.broadcasted_iota(jnp.int32, (64, 128), 1) < 64
     acts = []
     for side in range(2):
         pre = pe_ref[side] + sums[side]
@@ -223,6 +222,13 @@
         down = dg_ref[side * 256 : side * 256 + 256] + dot(spread.astype(BF16), ue_ref[side], NT)
         for p in range(NXY):
             down_ref[side, p] = down[p * 16 : p * 16 + 16]
+    return jnp.concatenate(acts, 1).astype(BF16)
+
+
+def edge_hidden(sums, pe_ref, hid_ref):
+    first = first_half((64, 128))
+    for side in range(2):
+        hidden = jnp.maximum(pe_ref[side] + sums[side], 0.0)
         tile = slice(384, 512) if side else slice(0, 128)
         for b in range(4):
             mine = hidden[:, b // 2 * 128 : b // 2 * 128 + 128]
@@ -230,7 +236,6 @@
                 mine = pltpu.roll(mine, 64, 1)
             old = hid_ref[b, :, tile].astype(F32)
             hid_ref[b, :, tile] = jnp.where(first != (side == 1), mine, old).astype(BF16)
-    return jnp.concatenate(acts, 1).astype(BF16)
 
 
 def put_rows(v_ref, at, rows):
@@ -348,7 +353,7 @@
         fill_outer(nb_ref, b, lo_ref, hi_ref, qe_ref)
     sums = outer_forward(w_ref, qe_ref)
 
-    acts = edge_planes(sums, pe_ref, ge_ref, ue_ref, hid_ref, dg_ref, down_ref)
+    acts = edge_planes(sums, pe_ref, ge_ref, ue_ref, dg_ref, down_ref)
     swap_down = remote(down_ref.at[1 - core], mate_down, cs.at[0], cr.at[0], sibling)
     swap_down.start()
     conv_gradient(acts, qe_ref, cg_ref, conv_ref)
@@ -377,6 +382,7 @@
     along[z] = total.astype(BF16)
     for peer in line:
         remote(along.at[z], along.at[z], zs.at[0], zr.at[0], peer).start()
+    edge_hidden(sums, pe_ref, hid_ref)
     swap_down.wait_send()
     swap_conv.wait_send()
     scattered.wait_send()

time: 39.2 us -> 39.2 us (level)
  no operation moved by 1% of the time
where the time goes in v10:
time: 39.2 us; the launch traced here: 39.1 us
  Pallas kernels  37.8 us (96%)
  between operations  1.29 us (3%)
    pallas_call x1, Pallas kernels, section(): pl.pallas_call(section_kernel, out_shape=(pltpu.VMEM((4, 64, 512), BF16),...  36.6 us
    pallas_call x1, Pallas kernels, unpack(): pl.pallas_call(unpack_kernel, out_shape=(jax.ShapeDtypeStruct((27, 64, 64...  1.13 us

profile of v10, /device:TPU:1, one launch (start us, length us, event | category | flops | bytes accessed | tf_op | source)
XLA Modules:
  0.0 39.1 jit_solution(3668155730664267348)
XLA Ops:
  1.3 36.6 %section.1 = (bf16[4,64,512]{2,1,0:T(8,128)(2,1)S(1)}, f32[32,48,128]{2,1,0:T(8,128)S(1)}) custom-call(s32[4,27]{1,0:T(4,128)} %nb_hbm.1, s32[1]{0:T(128)S(6)} %copy.9.cnt_hbm, bf16[4,64,512]{2,1,0:T(8,128)(2,1)} %f_hbm.1, bf16[4,64,128]{2,1,0:T(8,128)(2,1)} %g_hbm.1, bf16[27,64,64]{2,1,0:T(8,128)(2,1)} %cw_hbm.1, bf16[8,64,128]{2,1,0:T(8,128)(2,1)} %bitcast.4), custom_call_target="tpu_custom_call" | custom-call | tf_op jit(solution)/shard_map/section/pallas_call | solution.py:421
  37.9 1.1 %unpack.1 = (f32[27,64,64]{2,1,0:T(8,128)}, f32[32,16,128]{2,1,0:T(8,128)}, bf16[4,64,512]{2,1,0:T(8,128)(2,1)}) custom-call(f32[32,48,128]{2,1,0:T(8,128)S(1)} %get-tuple-element.8.v_ref, bf16[4,64,512]{2,1,0:T(8,128)(2,1)S(1)} %get-tuple-element.9.hid_ref), custom_call_target="tpu_custom_call" | custom-call | tf_op jit(solution)/shard_map/unpack/pallas_call | solution.py:479
